TPU v7x, 32 devices: a whole 2x2x4 slice. The times are simulated.
32 devices in a mesh: band: 8 (over y, x, core), grid: 4 (over z).
Axes of the slice: x: 2, y: 2, z: 4, core: 2. Of those that a mesh axis runs over, the one named last changes fastest.
Arguments:
- orbitals: float32 [16, 96, 9216], P('band', 'grid'), may hold values from -6 to 6
Outputs:
- exchange_images: float32 [16, 96, 9216], P('band', 'grid')
- projection: float32 [16, 2], P('band')
All inputs are finite; a program needn't handle non-finite values.
Results may differ from a plain program's by a relative error of at most 0.0003.
Values sent between devices are 32-bit elements; how exact they have to be, the bound alone decides.
A program may use at most 64 MiB of HBM per device.

v0:
```python
import math

import jax
import jax.numpy as jnp
from jax import lax
from jax.sharding import PartitionSpec as P

G = 96
STEPS = 2


cell_edge = 41.05
mixing = 0.25
highest = lax.Precision.HIGHEST


def passed_along(x, axis, by):
    length = lax.axis_size(axis)
    return lax.ppermute(x, axis, [(i, (i + by) % length) for i in range(length)])


def cas_table(length):
    position = jnp.arange(length, dtype=jnp.int32)
    phase = position[:, None] * position[None, :] % length
    angle = phase.astype(jnp.float32) * (2.0 * math.pi / length)
    return jnp.cos(angle) + jnp.sin(angle)


def folded_square(values, length):
    wrapped = jnp.minimum(values, length - values)
    return wrapped * wrapped


def shards(orbitals):
    band_count = orbitals.shape[0]
    slab_width = orbitals.shape[1]
    grid_count = lax.axis_size("grid")
    column_width = G // grid_count
    cas_values = cas_table(G)
    frequency = jnp.arange(G, dtype=jnp.int32)
    my_columns = lax.axis_index("grid") * column_width + jnp.arange(column_width, dtype=jnp.int32)
    squared = (
        folded_square(frequency, G)[:, None, None]
        + folded_square(my_columns, G)[None, :, None]
        + folded_square(frequency, G)[None, None, :]
    )
    coulomb = cell_edge * cell_edge / math.pi / float(G * G * G)
    kernel = jnp.where(
        squared > 0, coulomb / jnp.maximum(squared, 1).astype(jnp.float32), jnp.float32(0.0)
    )

    def column_solve(incoming):
        pair_count = incoming.shape[0]
        volume = incoming.reshape(pair_count, G, column_width, G)
        spectrum = jnp.einsum("pxyz,kx->pkyz", volume, cas_values, precision=highest) * kernel
        potential = jnp.einsum("pkyz,xk->pxyz", spectrum, cas_values, precision=highest)
        return potential.reshape(incoming.shape)

    def poisson_solve(density):
        pair_count = density.shape[0]
        volume = density.reshape(pair_count, slab_width, G, G)
        volume = jnp.einsum("pxyz,cz->pxyc", volume, cas_values, precision=highest)
        volume = jnp.einsum("pxyc,dy->pxdc", volume, cas_values, precision=highest)
        row_layout = volume.reshape(pair_count, slab_width, grid_count, column_width * G)
        column_result = column_solve(
            lax.all_to_all(row_layout, "grid", split_axis=2, concat_axis=1, tiled=True)
        )
        slab_result = lax.all_to_all(column_result, "grid", split_axis=1, concat_axis=2, tiled=True)
        volume = slab_result.reshape(pair_count, slab_width, G, G)
        volume = jnp.einsum("pxdc,yd->pxyc", volume, cas_values, precision=highest)
        volume = jnp.einsum("pxyc,zc->pxyz", volume, cas_values, precision=highest)
        return volume.reshape(pair_count, slab_width, G * G)

    def pair_products(visitor):
        return (orbitals[:, None] * visitor[None]).reshape(
            band_count * band_count, slab_width, G * G
        )

    visitors = []
    current = orbitals
    for hop_index in range(STEPS):
        current = passed_along(current, "band", 1)
        visitors.append(current)
    potentials = [poisson_solve(pair_products(visitor)) for visitor in visitors]
    own_sum = jnp.zeros_like(orbitals)
    returned_parts = []
    for potential, visitor in zip(potentials, visitors):
        shaped = potential.reshape(band_count, band_count, slab_width, G * G)
        own_sum = own_sum - mixing * jnp.sum(shaped * visitor[None], axis=1)
        returned_parts.append(-mixing * jnp.sum(shaped * orbitals[:, None], axis=0))
    carried = jnp.zeros_like(orbitals)
    for hop_index in reversed(range(STEPS)):
        carried = passed_along(carried + returned_parts[hop_index], "band", -1)
    images = own_sum + carried
    partial_value = jnp.einsum(
        "ir,jr->ij",
        orbitals.reshape(band_count, slab_width * G * G),
        images.reshape(band_count, slab_width * G * G),
        precision=highest,
    ) / float(G * G * G)
    intersection = lax.psum(partial_value, "grid")
    return (images, intersection)


def solution(mesh):
    return jax.shard_map(
        shards,
        mesh=mesh,
        in_specs=(P("band", "grid", None),),
        out_specs=(P("band", "grid", None), P("band", None)),
        check_vma=False,
    )
```

profile of v0, /device:TPU:0, one launch (start us, length us, event | category | flops | bytes accessed | tf_op | source)
XLA Modules:
  0.0 610.0 jit_solution(10676675656980913033)
XLA Ops:
  1.1 23.3 %collective-permute-done = f32[2,24,9216]{2,1,0:T(8,128)S(1)} collective-permute-done((f32[2,24,9216]{2,1,0:T(8,128)}, f32[2,24,9216]{2,1,0:T(8,128)S(1)}, u32[]{:S(2)}, u32[]{:S(2)}) %collective-permute-start) | collective-permute-done | bytes 1769504 | tf_op jit(solution)/shard_map/ppermute | solution.py:19
  25.6 1.8 broadcast_multiply_fusion.1
  27.5 3.6 mul.227
  31.1 6.3 %fusion.59 = f32[4,24,96,96]{3,2,1,0:T(8,128)S(1)} fusion(f32[4,24,96,96]{3,2,1,0:T(8,128)} %mul.227), kind=kOutput, calls=%fused_computation.59 | convolution fusion | flops 1019308032 | bytes 7077888 | tf_op jit(solution)/shard_map/pxyz,cz->pxyc/dot_general | solution.py:62
  37.4 6.1 %convolution_bitcast_fusion.1 = f32[4,24,96,96]{3,2,1,0:T(8,128)} fusion(f32[4,24,96,96]{3,2,1,0:T(8,128)S(1)} %fusion.59), kind=kOutput, calls=%fused_computation.23 | convolution fusion | flops 1019308032 | bytes 7077888 | tf_op jit(solution)/shard_map/pxyc,dy->pxdc/dot_general | solution.py:63
  43.5 4.5 reshape.102
  48.0 2.4 copy.15
  50.4 5.9 all-to-all-start
  56.4 1.3 fusion.27
  57.8 76.1 %all-to-all-done = f32[4,24,4,2304]{3,1,0,2:T(8,128)S(1)} async-done(((f32[4,24,4,2304]{3,1,0,2:T(8,128)}), f32[4,24,4,2304]{3,1,0,2:T(8,128)S(1)}, u32[]{:S(2)}, u32[]{:S(2)}) %all-to-all-start) | async-done | bytes 3538976 | tf_op jit(solution)/shard_map/all_to_all | solution.py:66
  133.9 2.1 copy.16
  136.0 6.2 %reshape.103 = f32[4,96,24,96]{3,2,1,0:T(8,128)} reshape(f32[4,4,24,1,2304]{4,2,1,0,3:T(8,128)} %copy.16) | data formatting | bytes 7077888 | tf_op jit(solution)/shard_map/reshape | solution.py:54
  142.2 8.0 %fusion.10 = f32[96,4,24,96]{3,0,2,1:T(8,128)S(1)} fusion(f32[4,96,24,96]{3,2,1,0:T(8,128)} %reshape.103), kind=kOutput, calls=%fused_computation.10 | convolution fusion | flops 1019308032 | bytes 7077888 | tf_op jit(solution)/shard_map/pxyz,kx->pkyz/dot_general | solution.py:55
  150.2 4.5 fusion.16
  154.7 4.9 copy.31
  159.6 5.7 reshape.112
  165.3 3.7 all-to-all-start.1
  169.1 78.5 %all-to-all-done.1 = f32[4,96,1,2304]{3,0,2,1:T(4,128)S(1)} async-done(((f32[4,96,1,2304]{3,0,2,1:T(4,128)}), f32[4,96,1,2304]{3,0,2,1:T(4,128)S(1)}, u32[]{:S(2)}, u32[]{:S(2)}) %all-to-all-start.1) | async-done | bytes 3538976 | tf_op jit(solution)/shard_map/all_to_all | solution.py:68
  247.6 4.1 copy.58
  251.7 6.9 %reshape.105 = f32[4,24,96,96]{3,2,1,0:T(8,128)} reshape(f32[4,24,4,1,2304]{4,2,1,0,3:T(4,128)} %bitcast.115) | data formatting | bytes 7077888 | tf_op jit(solution)/shard_map/reshape | solution.py:69
  258.6 6.4 %fusion.54 = f32[96,4,24,96]{3,0,2,1:T(8,128)S(1)} fusion(f32[4,24,96,96]{3,2,1,0:T(8,128)} %reshape.105), kind=kOutput, calls=%fused_computation.54 | convolution fusion | flops 1019308032 | bytes 7077888 | tf_op jit(solution)/shard_map/pxdc,yd->pxyc/dot_general | solution.py:70
  265.1 6.0 fusion.4
  271.0 6.2 %reshape_reshape.8 = f32[2,2,24,9216]{3,2,1,0:T(8,128)} reshape(f32[4,24,96,96]{3,2,1,0:T(8,128)} %fusion.4) | data formatting | bytes 7077888 | tf_op jit(solution)/shard_map/reshape;reshape | solution.py:88
  277.3 7.1 %multiply_reduce_fusion.3 = (f32[2,24,9216]{2,1,0:T(8,128)}, f32[2,24,9216]{2,1,0:T(8,128)}, f32[2,2,24,9216]{3,2,1,0:T(8,128)}) fusion(f32[2,2,24,9216]{3,2,1,0:T(8,128)} %reshape_reshape.8, f32[2,24,9216]{2,1,0:T(8,128)S(1)} %copy-done.4, f32[2,24,9216]{2,1,0:T(8,128)S(1)} %copy-done, f32[2,24,9216]{2,1,0:T(8,128)} %collective-permute-done.1), kind=kLoop, calls=%fused_computation.19 | loop fusion | flops 3538944 | bytes 15925248 | tf_op jit(solution)/shard_map/reduce_sum | solution.py:89
  284.4 5.8 mul.238
  290.2 6.3 %fusion.51 = f32[4,24,96,96]{3,2,1,0:T(8,128)S(1)} fusion(f32[4,24,96,96]{3,2,1,0:T(8,128)} %mul.238), kind=kOutput, calls=%fused_computation.51 | convolution fusion | flops 1019308032 | bytes 7077888 | tf_op jit(solution)/shard_map/pxyz,cz->pxyc/dot_general | solution.py:62
  296.6 6.4 %convolution_bitcast_fusion = f32[4,24,96,96]{3,2,1,0:T(8,128)} fusion(f32[4,24,96,96]{3,2,1,0:T(8,128)S(1)} %fusion.51), kind=kOutput, calls=%fused_computation.22 | convolution fusion | flops 1019308032 | bytes 7077888 | tf_op jit(solution)/shard_map/pxyc,dy->pxdc/dot_general | solution.py:63
  302.9 5.7 reshape.106
  308.7 2.7 copy.21
  311.4 81.2 %all_to_all.60 = f32[4,24,4,2304]{3,1,0,2:T(8,128)S(1)} all-to-all(f32[4,24,4,2304]{3,1,0,2:T(8,128)S(1)} %copy.21), channel_id=1, replica_groups=mesh['band'=8,'grid'=4] {'grid'}, dimensions={2} | all-to-all | bytes 7077888 | tf_op jit(solution)/shard_map/all_to_all | solution.py:66
  392.6 2.1 copy.22
  394.6 6.2 %reshape.107 = f32[4,96,24,96]{3,2,1,0:T(8,128)} reshape(f32[4,4,24,1,2304]{4,2,1,0,3:T(8,128)} %copy.22) | data formatting | bytes 7077888 | tf_op jit(solution)/shard_map/reshape | solution.py:54
  400.8 7.8 %fusion.8 = f32[96,4,24,96]{3,0,2,1:T(8,128)S(1)} fusion(f32[4,96,24,96]{3,2,1,0:T(8,128)} %reshape.107), kind=kOutput, calls=%fused_computation.8 | convolution fusion | flops 1019308032 | bytes 7077888 | tf_op jit(solution)/shard_map/pxyz,kx->pkyz/dot_general | solution.py:55
  408.7 4.5 fusion.19
  413.3 4.9 copy.32
  418.1 5.7 reshape.113
  423.9 82.0 %all_to_all.61 = f32[4,96,1,2304]{3,0,2,1:T(4,128)S(1)} all-to-all(f32[4,96,1,2304]{3,0,2,1:T(4,128)} %reshape.113), channel_id=1, replica_groups=mesh['band'=8,'grid'=4] {'grid'}, dimensions={1} | all-to-all | bytes 7077888 | tf_op jit(solution)/shard_map/all_to_all | solution.py:68
  505.9 4.1 copy.57
  509.9 6.8 %reshape.109 = f32[4,24,96,96]{3,2,1,0:T(8,128)} reshape(f32[4,24,4,1,2304]{4,2,1,0,3:T(4,128)} %bitcast.116) | data formatting | bytes 7077888 | tf_op jit(solution)/shard_map/reshape | solution.py:69
  516.7 6.4 %fusion.46 = f32[96,4,24,96]{3,0,2,1:T(8,128)S(1)} fusion(f32[4,24,96,96]{3,2,1,0:T(8,128)} %reshape.109), kind=kOutput, calls=%fused_computation.46 | convolution fusion | flops 1019308032 | bytes 7077888 | tf_op jit(solution)/shard_map/pxdc,yd->pxyc/dot_general | solution.py:70
  523.2 6.0 fusion
  529.1 6.1 reshape_reshape.9
  535.2 3.8 multiply_reduce_fusion.2
  539.3 20.0 %collective-permute-done.2 = f32[2,24,9216]{2,1,0:T(8,128)S(1)} collective-permute-done((f32[2,24,9216]{2,1,0:T(8,128)S(1)}, f32[2,24,9216]{2,1,0:T(8,128)S(1)}, u32[]{:S(2)}, u32[]{:S(2)}) %collective-permute-start.2) | collective-permute-done | bytes 1769504 | tf_op jit(solution)/shard_map/ppermute | solution.py:19
  559.6 3.1 collective-permute-start.3
  562.6 20.0 %collective-permute-done.3 = f32[2,24,9216]{2,1,0:T(8,128)S(1)} collective-permute-done((f32[2,24,9216]{2,1,0:T(8,128)S(1)}, f32[2,24,9216]{2,1,0:T(8,128)S(1)}, u32[]{:S(2)}, u32[]{:S(2)}) %collective-permute-start.3) | collective-permute-done | bytes 1769504 | tf_op jit(solution)/shard_map/ppermute | solution.py:19
  583.0 16.2 %fusion.38 = f32[2,2]{0,1:T(2,128)S(1)} fusion(f32[2,24,9216]{2,1,0:T(8,128)S(1)} %copy-done, f32[2,24,9216]{2,1,0:T(8,128)S(1)} %subtract_add_fusion), kind=kOutput, calls=%fused_computation.40 | convolution fusion | flops 10616836 | bytes 3538960 | tf_op jit(solution)/shard_map/ir,jr->ij/dot_general | solution.py:95
  599.2 9.9 %psum.7 = f32[2,2]{0,1:T(2,128)S(1)} all-reduce(f32[2,2]{0,1:T(2,128)S(1)} %fusion.38), channel_id=1, replica_groups=mesh['band'=8,'grid'=4] {'grid'}, use_global_device_ids=true, to_apply=%region_4.5 | all-reduce | flops 4 | bytes 32 | tf_op jit(solution)/shard_map/psum | solution.py:101
  (27 shorter events, 3.3 us)
Async XLA Ops:
  0.6 23.8 %collective-permute-start = (f32[2,24,9216]{2,1,0:T(8,128)}, f32[2,24,9216]{2,1,0:T(8,128)S(1)}, u32[]{:S(2)}, u32[]{:S(2)}) collective-permute-start(f32[2,24,9216]{2,1,0:T(8,128)} %param.1), channel_id=1, source_target_pairs={{0,4},{4,8},{8,12},{12,16},{16,20},{20,24},{24,28},{28,0},{1,5},{5... | collective-permute-start | bytes 5308424 | tf_op jit(solution)/shard_map/ppermute | solution.py:19
  24.4 1.2 copy-start.3
  50.4 83.5 %all-to-all-start = ((f32[4,24,4,2304]{3,1,0,2:T(8,128)}), f32[4,24,4,2304]{3,1,0,2:T(8,128)S(1)}, u32[]{:S(2)}, u32[]{:S(2)}) async-start(f32[4,24,4,2304]{3,1,0,2:T(8,128)} %copy.15), calls=%async_computation | async-start | bytes 7077888 | tf_op jit(solution)/shard_map/all_to_all | solution.py:66
  142.2 8.0 %copy-start.1 = (f32[96,24,96]{2,0,1:T(8,128)S(1)}, f32[96,24,96]{2,0,1:T(8,128)}, u32[]{:S(2)}) copy-start(f32[96,24,96]{2,0,1:T(8,128)} %fusion.27) | copy-start | bytes 2654212
  165.3 82.3 %all-to-all-start.1 = ((f32[4,96,1,2304]{3,0,2,1:T(4,128)}), f32[4,96,1,2304]{3,0,2,1:T(4,128)S(1)}, u32[]{:S(2)}, u32[]{:S(2)}) async-start(f32[4,96,1,2304]{3,0,2,1:T(4,128)} %reshape.112), calls=%async_computation.1 | async-start | bytes 7077888 | tf_op jit(solution)/shard_map/all_to_all | solution.py:68
  169.1 108.2 %collective-permute-start.1 = (f32[2,24,9216]{2,1,0:T(8,128)}, f32[2,24,9216]{2,1,0:T(8,128)}, u32[]{:S(2)}, u32[]{:S(2)}) collective-permute-start(f32[2,24,9216]{2,1,0:T(8,128)} %copy-done.3), channel_id=1, source_target_pairs={{0,4},{4,8},{8,12},{12,16},{16,20},{20,24},{24,28},{28,0},{1,5},{5... | collective-permute-start | bytes 5308424 | tf_op jit(solution)/shard_map/ppermute | solution.py:19
  271.0 6.2 %copy-start = (f32[2,24,9216]{2,1,0:T(8,128)S(1)}, f32[2,24,9216]{2,1,0:T(8,128)}, u32[]{:S(2)}) copy-start(f32[2,24,9216]{2,1,0:T(8,128)} %param.1) | copy-start | bytes 5308420
  271.0 6.2 %copy-start.4 = (f32[2,24,9216]{2,1,0:T(8,128)S(1)}, f32[2,24,9216]{2,1,0:T(8,128)}, u32[]{:S(2)}) copy-start(f32[2,24,9216]{2,1,0:T(8,128)} %copy-done.3) | copy-start | bytes 5308420
  400.8 7.8 %copy-start.2 = (f32[96,24,96]{2,0,1:T(8,128)S(1)}, f32[96,24,96]{2,0,1:T(8,128)}, u32[]{:S(2)}) copy-start(f32[96,24,96]{2,0,1:T(8,128)} %fusion.27) | copy-start | bytes 2654212
  539.1 20.2 %copy-start.6 = (f32[2,24,9216]{2,1,0:T(8,128)S(1)}, f32[2,24,9216]{2,1,0:T(8,128)}, u32[]{:S(2)}) copy-start(f32[2,24,9216]{2,1,0:T(8,128)} %get-tuple-element.9) | copy-start | bytes 5308420
  539.2 43.5 %copy-start.5 = (f32[2,24,9216]{2,1,0:T(8,128)S(1)}, f32[2,24,9216]{2,1,0:T(8,128)}, u32[]{:S(2)}) copy-start(f32[2,24,9216]{2,1,0:T(8,128)} %get-tuple-element.8) | copy-start | bytes 5308420
  539.2 20.1 %collective-permute-start.2 = (f32[2,24,9216]{2,1,0:T(8,128)S(1)}, f32[2,24,9216]{2,1,0:T(8,128)S(1)}, u32[]{:S(2)}, u32[]{:S(2)}) collective-permute-start(f32[2,24,9216]{2,1,0:T(8,128)S(1)} %broadcast_multiply_fusion.2), channel_id=1, source_target_pairs={{0,28},{4,0},{8,4},{12,8},{16,12},{20,16},{24,20},{28,24},{1,29},{... | collective-permute-start | bytes 5308424 | tf_op jit(solution)/shard_map/ppermute | solution.py:19
  559.6 23.1 %collective-permute-start.3 = (f32[2,24,9216]{2,1,0:T(8,128)S(1)}, f32[2,24,9216]{2,1,0:T(8,128)S(1)}, u32[]{:S(2)}, u32[]{:S(2)}) collective-permute-start(f32[2,24,9216]{2,1,0:T(8,128)S(1)} %multiply_add_fusion), channel_id=1, source_target_pairs={{0,28},{4,0},{8,4},{12,8},{16,12},{20,16},{24,20},{28,24},{1,29},{... | collective-permute-start | bytes 5308424 | tf_op jit(solution)/shard_map/ppermute | solution.py:19
  583.0 26.8 %copy-start.7 = (f32[2,24,9216]{2,1,0:T(8,128)}, f32[2,24,9216]{2,1,0:T(8,128)S(1)}, u32[]{:S(2)}) copy-start(f32[2,24,9216]{2,1,0:T(8,128)S(1)} %subtract_add_fusion) | copy-start | bytes 5308420
where the time goes:
time: 617 us; the launch traced here: 610 us
  waiting for transfers between devices  218 us (35%)
  blocking collectives  173 us (28%)
  local copies, waits for them, and re-layouts  98.5 us (16%)
  matrix products  91.1 us (15%)
  other arithmetic  14.9 us (2%)
  starting transfers between devices  13.3 us (2%)
    all_to_all x1, blocking collectives, poisson_solve(): lax.all_to_all(column_result, 'grid', split_axis=1, concat_axis=2, tiled=...  82 us
    all_to_all x1, blocking collectives, poisson_solve(): lax.all_to_all(row_layout, 'grid', split_axis=2, concat_axis=1, tiled=True)  81.2 us
    all_to_all x1, waiting for transfers between devices, poisson_solve(): lax.all_to_all(column_result, 'grid', split_axis=1, concat_axis=2, tiled=...  78.5 us
    all_to_all x1, waiting for transfers between devices, poisson_solve(): lax.all_to_all(row_layout, 'grid', split_axis=2, concat_axis=1, tiled=True)  76.1 us
    ppermute x4, waiting for transfers between devices, passed_along(): lax.ppermute(x, axis, [(i, (i + by) % length) for i in range(length)])  63.4 us
    reshape x4, local copies, waits for them, and re-layouts, column_solve(): return potential.reshape(incoming.shape)  21.2 us
    dot_general x1, matrix products, shards(): jnp.einsum('ir,jr->ij', orbitals.reshape(band_count, slab_width * G * G),...  16.2 us
    dot_general x2, matrix products, column_solve(): jnp.einsum('pxyz,kx->pkyz', volume, cas_values, precision=highest) * kernel  15.8 us
  transfers between devices with their start and end apart: 6, of which 5 were waited for; matrix products, arithmetic and copies ran while one was open for 5% of the time, Pallas kernels for 0%

commit v1 on v0

v1 whole, which is shorter than its diff:
```python
import math

import jax
import jax.numpy as jnp
from jax import lax
from jax.sharding import PartitionSpec as P

G = 96
STEPS = 2


cell_edge = 41.05
mixing = 0.25
highest = lax.Precision.HIGHEST
split = lax.Precision.HIGH


def passed_along(x, axis, by):
    length = lax.axis_size(axis)
    return lax.ppermute(x, axis, [(i, (i + by) % length) for i in range(length)])


def cas_table(length):
    position = jnp.arange(length, dtype=jnp.int32)
    phase = position[:, None] * position[None, :] % length
    angle = phase.astype(jnp.float32) * (2.0 * math.pi / length)
    return jnp.cos(angle) + jnp.sin(angle)


def folded_square(values, length):
    wrapped = jnp.minimum(values, length - values)
    return wrapped * wrapped


def shards(orbitals):
    band_count = orbitals.shape[0]
    slab_width = orbitals.shape[1]
    grid_count = lax.axis_size("grid")
    column_width = G // grid_count
    pairs = band_count * band_count
    lanes = pairs * G
    cas_values = cas_table(G)
    lane_table = jnp.kron(jnp.eye(pairs, dtype=jnp.float32), cas_values)
    frequency = jnp.arange(G, dtype=jnp.int32)
    my_columns = lax.axis_index("grid") * column_width + jnp.arange(column_width, dtype=jnp.int32)
    squared = (
        folded_square(frequency, G)[:, None, None]
        + folded_square(my_columns, G)[None, :, None]
        + folded_square(frequency, G)[None, None, :]
    )
    coulomb = cell_edge * cell_edge / math.pi / float(G * G * G)
    kernel = jnp.where(
        squared > 0, coulomb / jnp.maximum(squared, 1).astype(jnp.float32), jnp.float32(0.0)
    )
    kernel = jnp.tile(kernel, (1, 1, pairs))

    def forward(density):
        volume = jnp.einsum("xyl,lm->xym", density, lane_table, precision=split)
        volume = jnp.einsum("xym,dy->xdm", volume, cas_values, precision=split)
        return volume.reshape(slab_width, grid_count, column_width, lanes).transpose(1, 0, 2, 3)

    def column_solve(parts):
        volume = parts.reshape(G, column_width, lanes)
        spectrum = jnp.einsum("kx,xyl->kyl", cas_values, volume, precision=split) * kernel
        potential = jnp.einsum("xk,kyl->xyl", cas_values, spectrum, precision=split)
        return potential.reshape(parts.shape)

    def backward(parts):
        volume = parts.transpose(1, 0, 2, 3).reshape(slab_width, G, lanes)
        volume = jnp.einsum("xdm,yd->xym", volume, cas_values, precision=split)
        return jnp.einsum("xym,ml->xyl", volume, lane_table, precision=split)

    def exchange(parts):
        return lax.all_to_all(parts, "grid", split_axis=0, concat_axis=0, tiled=True)

    cubes = orbitals.reshape(band_count, slab_width, G, G)
    own = [cubes[i] for i in range(band_count)]
    wide_own = jnp.concatenate([own[i] for i in range(band_count) for _ in range(band_count)], axis=2)

    visitors = []
    current = jnp.concatenate(own, axis=2)
    for hop_index in range(STEPS):
        current = passed_along(current, "band", 1)
        visitors.append(current)
    sent = [
        exchange(forward(wide_own * jnp.concatenate([visitor] * band_count, axis=2)))
        for visitor in visitors
    ]
    returned = [exchange(column_solve(parts)) for parts in sent]
    own_sum = [0.0] * band_count
    returned_parts = []
    for parts, visitor in zip(returned, visitors):
        potential = backward(parts)
        to_own = potential * jnp.concatenate([visitor] * band_count, axis=2)
        to_visitor = potential * wide_own
        back = []
        for j in range(band_count):
            total = 0.0
            for i in range(band_count):
                at = (i * band_count + j) * G
                total = total + to_visitor[:, :, at:at + G]
            back.append(total)
        for i in range(band_count):
            for j in range(band_count):
                at = (i * band_count + j) * G
                own_sum[i] = own_sum[i] + to_own[:, :, at:at + G]
        returned_parts.append(jnp.concatenate(back, axis=2))
    carried = returned_parts[STEPS - 1]
    for hop_index in reversed(range(STEPS)):
        carried = passed_along(carried, "band", -1)
        if hop_index:
            carried = carried + returned_parts[hop_index - 1]
    images = -mixing * (
        jnp.stack(own_sum) + jnp.stack([carried[:, :, i * G:(i + 1) * G] for i in range(band_count)])
    )
    partial_value = jnp.einsum(
        "ixyz,jxyz->ij", cubes, images, precision=highest
    ) / float(G * G * G)
    intersection = lax.psum(partial_value, "grid")
    return (images.reshape(orbitals.shape), intersection)


def solution(mesh):
    return jax.shard_map(
        shards,
        mesh=mesh,
        in_specs=(P("band", "grid", None),),
        out_specs=(P("band", "grid", None), P("band", None)),
        check_vma=False,
    )
```

time: 617 us -> 521 us (0.84)
  blocking collectives: 173 us -> 9.83 us
  waiting for transfers between devices: 218 us -> 333 us
  local copies, waits for them, and re-layouts: 98.5 us -> 43.3 us
  starting transfers between devices: 13.3 us -> 23.6 us
    all_to_all x2 -> x0, blocking collectives: 163 us -> none  [the longest x1 82 us: poisson_solve(): lax.all_to_all(column_result, 'grid', split_axis=1, concat_axis=2, tiled=...]
    all_to_all x2 -> x4, waiting for transfers between devices: 155 us -> 238 us  [exchange(): lax.all_to_all(parts, 'grid', split_axis=0, concat_axis=0, tiled=True)]
    reshape x12 -> x5, local copies, waits for them, and re-layouts: 62.6 us -> 15 us  [the longest x2 7.72 us: column_solve(): return potential.reshape(parts.shape)]
    ppermute x4, waiting for transfers between devices: 63.4 us -> 95.7 us  [passed_along(): lax.ppermute(x, axis, [(i, (i + by) % length) for i in range(length)])]
    reduce_sum x2 -> x0, other arithmetic: 11 us -> none  [shards(): own_sum = own_sum - mixing * jnp.sum(shaped * visitor[None], axis=1)]
    add x2 -> x5, other arithmetic: 0.54 us -> 10.7 us  [the longest x1 6.38 us: shards(): own_sum[i] = own_sum[i] + to_own[:, :, at:at + G]]
    all_to_all x2 -> x4, starting transfers between devices: 9.64 us -> 19.8 us  [exchange(): lax.all_to_all(parts, 'grid', split_axis=0, concat_axis=0, tiled=True)]
    all_to_all x4 -> x2, local copies, waits for them, and re-layouts: 12.2 us -> 2.85 us  [exchange(): lax.all_to_all(parts, 'grid', split_axis=0, concat_axis=0, tiled=True)]
  transfers between devices with their start and end apart: 6 -> 8, of which waited for: 5 -> 8; matrix products, arithmetic and copies ran while one was open for 5% -> 12% of each run, Pallas kernels for 0% -> 0%
where the time goes in v1:
time: 521 us; the launch traced here: 515 us
  waiting for transfers between devices  333 us (64%)
  matrix products  85 us (16%)
  local copies, waits for them, and re-layouts  43.3 us (8%)
  starting transfers between devices  23.6 us (5%)
  other arithmetic  18.4 us (4%)
  blocking collectives  9.83 us (2%)
    all_to_all x4, waiting for transfers between devices, exchange(): lax.all_to_all(parts, 'grid', split_axis=0, concat_axis=0, tiled=True)  238 us
    ppermute x4, waiting for transfers between devices, passed_along(): lax.ppermute(x, axis, [(i, (i + by) % length) for i in range(length)])  95.7 us
    dot_general x1, matrix products, shards(): jnp.einsum('ixyz,jxyz->ij', cubes, images, precision=highest)  32.5 us
    all_to_all x4, starting transfers between devices, exchange(): lax.all_to_all(parts, 'grid', split_axis=0, concat_axis=0, tiled=True)  19.8 us
    dot_general x2, matrix products, forward(): volume = jnp.einsum('xyl,lm->xym', density, lane_table, precision=split)  15.5 us
    dot_general x2, matrix products, backward(): return jnp.einsum('xym,ml->xyl', volume, lane_table, precision=split)  15 us
  transfers between devices with their start and end apart: 8, of which 8 were waited for; matrix products, arithmetic and copies ran while one was open for 12% of the time, Pallas kernels for 0%

profile of v1, /device:TPU:0, one launch (start us, length us, event | category | flops | bytes accessed | tf_op | source)
XLA Modules:
  0.0 514.5 jit_solution(7963124499996805817)
XLA Ops:
  0.6 1.6 fusion.89
  3.1 2.1 pad_maximum_fusion.5
  7.0 1.5 reshape.151
  8.5 26.9 %collective-permute-done = f32[24,96,192]{2,1,0:T(8,128)} collective-permute-done((f32[24,96,192]{2,1,0:T(8,128)}, f32[24,96,192]{2,1,0:T(8,128)}, u32[]{:S(2)}, u32[]{:S(2)}) %collective-permute-start) | collective-permute-done | bytes 1769504 | tf_op jit(solution)/shard_map/ppermute | solution.py:20
  35.4 7.3 %fusion.14 = f32[24,96,384]{2,1,0:T(8,128)S(1)} fusion(f32[384,384,1]{1,0,2:T(8,128)S(1)} %reshape.151, f32[24,96,192]{2,1,0:T(8,128)} %collective-permute-done, f32[24,96,96]{2,1,0:T(8,128)S(1)} %squeeze.7, f32[24,96,96]{2,1,0:T(8,128)S(1)} %squeeze.6), kind=kOutput, calls=%fused_computation.19 | convolution fusion | flops 2042855424 | bytes 7667712 | tf_op jit(solution)/shard_map/xyl,lm->xym/dot_general | solution.py:58
  42.8 2.0 fusion.55
  44.8 2.0 copy.48
  46.8 5.6 %all-to-all-start = ((f32[4,24,24,384]{3,2,1,0:T(8,128)}), f32[4,24,24,384]{3,2,1,0:T(8,128)S(1)}, u32[]{:S(2)}, u32[]{:S(2)}) async-start(f32[4,24,24,384]{3,2,1,0:T(8,128)} %bitcast.75), calls=%async_computation | async-start | bytes 7077888 | tf_op jit(solution)/shard_map/all_to_all | solution.py:74
  52.6 29.4 %collective-permute-done.1 = f32[24,96,192]{2,1,0:T(8,128)S(1)} collective-permute-done((f32[24,96,192]{2,1,0:T(8,128)}, f32[24,96,192]{2,1,0:T(8,128)S(1)}, u32[]{:S(2)}, u32[]{:S(2)}) %collective-permute-start.1) | collective-permute-done | bytes 1769504 | tf_op jit(solution)/shard_map/ppermute | solution.py:20
  82.0 8.2 %fusion.10 = f32[24,96,384]{2,1,0:T(8,128)S(1)} fusion(f32[384,384,1]{1,0,2:T(8,128)} %copy-done.7, f32[24,96,192]{2,1,0:T(8,128)S(1)} %collective-permute-done.1, f32[24,96,96]{2,1,0:T(8,128)} %copy-done.3, f32[24,96,96]{2,1,0:T(8,128)} %copy-done.1), kind=kOutput, calls=%fused_computation.15 | convolution fusion | flops 2042855424 | bytes 7667712 | tf_op jit(solution)/shard_map/xyl,lm->xym/dot_general | solution.py:58
  90.1 2.0 fusion.49
  92.2 2.0 copy.47
  94.2 35.7 %all-to-all-done = f32[4,24,24,384]{3,2,1,0:T(8,128)S(1)} async-done(((f32[4,24,24,384]{3,2,1,0:T(8,128)}), f32[4,24,24,384]{3,2,1,0:T(8,128)S(1)}, u32[]{:S(2)}, u32[]{:S(2)}) %all-to-all-start) | async-done | bytes 3538976 | tf_op jit(solution)/shard_map/all_to_all | solution.py:74
  129.9 1.8 copy-done
  131.7 5.1 all-to-all-start.2
  137.2 3.0 tile.4
  140.2 4.3 tile.10
  144.6 4.2 fusion.6
  148.8 1.9 fusion.12
  150.7 3.8 copy.15
  154.5 60.9 %all-to-all-done.2 = f32[4,24,24,384]{3,2,1,0:T(8,128)} async-done(((f32[4,24,24,384]{3,2,1,0:T(8,128)}), f32[4,24,24,384]{3,2,1,0:T(8,128)}, u32[]{:S(2)}, u32[]{:S(2)}) %all-to-all-start.2) | async-done | bytes 3538976 | tf_op jit(solution)/shard_map/all_to_all | solution.py:74
  215.4 5.2 %all-to-all-start.1 = ((f32[4,24,24,384]{3,2,1,0:T(8,128)}), f32[4,24,24,384]{3,2,1,0:T(8,128)}, u32[]{:S(2)}, u32[]{:S(2)}) async-start(f32[4,24,24,384]{3,2,1,0:T(8,128)} %copy.15), calls=%async_computation.1 | async-start | bytes 7077888 | tf_op jit(solution)/shard_map/all_to_all | solution.py:74
  220.6 4.2 fusion.4
  224.8 1.9 fusion.8
  226.7 3.9 copy.19
  230.7 68.6 %all-to-all-done.1 = f32[4,24,24,384]{3,2,1,0:T(8,128)} async-done(((f32[4,24,24,384]{3,2,1,0:T(8,128)}), f32[4,24,24,384]{3,2,1,0:T(8,128)}, u32[]{:S(2)}, u32[]{:S(2)}) %all-to-all-start.1) | async-done | bytes 3538976 | tf_op jit(solution)/shard_map/all_to_all | solution.py:74
  299.2 3.9 all-to-all-start.3
  303.2 2.4 copy.16
  305.6 3.7 fusion.51
  309.3 72.4 %all-to-all-done.3 = f32[4,24,24,384]{3,2,1,0:T(8,128)S(1)} async-done(((f32[4,24,24,384]{3,2,1,0:T(8,128)}), f32[4,24,24,384]{3,2,1,0:T(8,128)S(1)}, u32[]{:S(2)}, u32[]{:S(2)}) %all-to-all-start.3) | async-done | bytes 3538976 | tf_op jit(solution)/shard_map/all_to_all | solution.py:74
  382.1 2.0 fusion.45
  384.2 5.2 %fusion = f32[24,96,384]{2,1,0:T(8,128)} fusion(f32[384,384,1]{1,0,2:T(8,128)S(1)} %copy-done.8, f32[96,24,384]{2,0,1:T(8,128)S(1)} %fusion.45), kind=kOutput, calls=%fused_computation.3 | convolution fusion | flops 2038431744 | bytes 7667712 | tf_op jit(solution)/shard_map/xym,ml->xyl/dot_general | solution.py:71
  389.4 9.8 %fusion.41 = (f32[24,96,384]{2,1,0:T(8,128)S(1)}, f32[24,96,384]{2,1,0:T(8,128)S(1)}, f32[24,96,384]{2,1,0:T(8,128)}, f32[24,96,384]{2,1,0:T(8,128)S(1)}) fusion(f32[24,96,96]{2,1,0:T(8,128)S(1)} %copy-done.4, f32[24,96,96]{2,1,0:T(8,128)S(1)} %copy-done.2, f32[24,96,192]{2,1,0:T(8,128)} %collective-permute-done, f32[24,96,384]{2,1,0:T(8,128)} %fusion, ...), kind=kOutput, calls=%fused_computation.51 | convolution fusion | flops 2046394368 | bytes 27131904 | tf_op jit(solution)/shard_map/xym,ml->xyl/dot_general | solution.py:71
  402.2 25.4 %collective-permute-done.2 = f32[24,96,192]{2,1,0:T(8,128)S(1)} collective-permute-done((f32[24,96,192]{2,1,0:T(8,128)S(1)}, f32[24,96,192]{2,1,0:T(8,128)S(1)}, u32[]{:S(2)}, u32[]{:S(2)}) %collective-permute-start.2) | collective-permute-done | bytes 1769504 | tf_op jit(solution)/shard_map/ppermute | solution.py:20
  427.6 2.2 maximum_add_fusion
  429.8 2.8 collective-permute-start.3
  432.6 3.3 reshape.150
  435.9 6.4 %slice_add_fusion.7 = (f32[24,96,96]{2,1,0:T(8,128)}, f32[24,96,96]{2,1,0:T(8,128)}) fusion(f32[24,96,384]{2,1,0:T(8,128)} %get-tuple-element.22, f32[24,96,384]{2,1,0:T(8,128)S(1)} %get-tuple-element.13), kind=kLoop, calls=%fused_computation.45 | loop fusion | flops 1327104 | bytes 8847360 | tf_op jit(solution)/shard_map/add | solution.py:106
  442.3 2.9 stack.30
  445.2 14.1 %collective-permute-done.3 = f32[24,96,192]{2,1,0:T(8,128)} collective-permute-done((f32[24,96,192]{2,1,0:T(8,128)}, f32[24,96,192]{2,1,0:T(8,128)}, u32[]{:S(2)}, u32[]{:S(2)}) %collective-permute-start.3) | collective-permute-done | bytes 1769504 | tf_op jit(solution)/shard_map/ppermute | solution.py:20
  459.3 2.7 slice_bitcast_fusion.1
  462.5 1.2 copy-done.12
  463.6 32.5 %fusion.36 = f32[2,2]{0,1:T(2,128)S(1)} fusion(f32[2,24,96,96]{3,2,1,0:T(8,128)S(1)} %copy-done.12, f32[2,24,96,96]{3,2,1,0:T(8,128)S(1)} %fusion.18), kind=kOutput, calls=%fused_computation.50 | convolution fusion | flops 10616836 | bytes 3538960 | tf_op jit(solution)/shard_map/ixyz,jxyz->ij/dot_general | solution.py:116
  496.1 1.6 stack.31
  497.7 9.8 %psum.7 = f32[2,2]{0,1:T(2,128)S(1)} all-reduce(f32[2,2]{0,1:T(2,128)S(1)} %fusion.36), channel_id=1, replica_groups=mesh['band'=8,'grid'=4] {'grid'}, use_global_device_ids=true, to_apply=%region_0.1 | all-reduce | flops 4 | bytes 32 | tf_op jit(solution)/shard_map/psum | solution.py:119
  508.2 1.7 stack.33
  509.9 1.6 stack.34
  511.5 2.8 fusion.22
  (42 shorter events, 7.9 us)
Async XLA Ops:
  2.7 32.8 %copy-start.1 = (f32[24,96,96]{2,1,0:T(8,128)}, f32[24,96,96]{2,1,0:T(8,128)S(1)}, u32[]{:S(2)}) copy-start(f32[24,96,96]{2,1,0:T(8,128)S(1)} %squeeze.6) | copy-start | bytes 2654212
  3.1 32.3 %copy-start.3 = (f32[24,96,96]{2,1,0:T(8,128)}, f32[24,96,96]{2,1,0:T(8,128)S(1)}, u32[]{:S(2)}) copy-start(f32[24,96,96]{2,1,0:T(8,128)S(1)} %squeeze.7) | copy-start | bytes 2654212
  5.3 30.2 %collective-permute-start = (f32[24,96,192]{2,1,0:T(8,128)}, f32[24,96,192]{2,1,0:T(8,128)}, u32[]{:S(2)}, u32[]{:S(2)}) collective-permute-start(f32[24,96,192]{2,1,0:T(8,128)} %pad_maximum_fusion.5), channel_id=1, source_target_pairs={{0,4},{4,8},{8,12},{12,16},{16,20},{20,24},{24,28},{28,0},{1,5},{5... | collective-permute-start | bytes 5308424 | tf_op jit(solution)/shard_map/ppermute | solution.py:20
  8.5 34.2 %copy-start.7 = (f32[384,384,1]{1,0,2:T(8,128)}, f32[384,384,1]{1,0,2:T(8,128)S(1)}, u32[]{:S(2)}) copy-start(f32[384,384,1]{1,0,2:T(8,128)S(1)} %reshape.151) | copy-start | bytes 1769476
  46.8 83.1 %all-to-all-start = ((f32[4,24,24,384]{3,2,1,0:T(8,128)}), f32[4,24,24,384]{3,2,1,0:T(8,128)S(1)}, u32[]{:S(2)}, u32[]{:S(2)}) async-start(f32[4,24,24,384]{3,2,1,0:T(8,128)} %bitcast.75), calls=%async_computation | async-start | bytes 7077888 | tf_op jit(solution)/shard_map/all_to_all | solution.py:74
  52.4 29.6 %collective-permute-start.1 = (f32[24,96,192]{2,1,0:T(8,128)}, f32[24,96,192]{2,1,0:T(8,128)S(1)}, u32[]{:S(2)}, u32[]{:S(2)}) collective-permute-start(f32[24,96,192]{2,1,0:T(8,128)} %collective-permute-done), channel_id=1, source_target_pairs={{0,4},{4,8},{8,12},{12,16},{16,20},{20,24},{24,28},{28,0},{1,5},{5... | collective-permute-start | bytes 5308424 | tf_op jit(solution)/shard_map/ppermute | solution.py:20
  82.0 8.2 %copy-start.11 = (f32[24,96,192]{2,1,0:T(8,128)}, f32[24,96,192]{2,1,0:T(8,128)S(1)}, u32[]{:S(2)}) copy-start(f32[24,96,192]{2,1,0:T(8,128)S(1)} %collective-permute-done.1) | copy-start | bytes 5308420
  129.9 1.8 copy-start
  131.7 83.7 %all-to-all-start.2 = ((f32[4,24,24,384]{3,2,1,0:T(8,128)}), f32[4,24,24,384]{3,2,1,0:T(8,128)}, u32[]{:S(2)}, u32[]{:S(2)}) async-start(f32[4,24,24,384]{3,2,1,0:T(8,128)} %bitcast.74), calls=%async_computation.2 | async-start | bytes 7077888 | tf_op jit(solution)/shard_map/all_to_all | solution.py:74
  215.4 83.9 %all-to-all-start.1 = ((f32[4,24,24,384]{3,2,1,0:T(8,128)}), f32[4,24,24,384]{3,2,1,0:T(8,128)}, u32[]{:S(2)}, u32[]{:S(2)}) async-start(f32[4,24,24,384]{3,2,1,0:T(8,128)} %copy.15), calls=%async_computation.1 | async-start | bytes 7077888 | tf_op jit(solution)/shard_map/all_to_all | solution.py:74
  299.2 82.5 %all-to-all-start.3 = ((f32[4,24,24,384]{3,2,1,0:T(8,128)}), f32[4,24,24,384]{3,2,1,0:T(8,128)S(1)}, u32[]{:S(2)}, u32[]{:S(2)}) async-start(f32[4,24,24,384]{3,2,1,0:T(8,128)} %copy.19), calls=%async_computation.3 | async-start | bytes 7077888 | tf_op jit(solution)/shard_map/all_to_all | solution.py:74
  382.1 2.0 copy-start.8
  384.2 5.2 %copy-start.2 = (f32[24,96,96]{2,1,0:T(8,128)S(1)}, f32[24,96,96]{2,1,0:T(8,128)}, u32[]{:S(2)}) copy-start(f32[24,96,96]{2,1,0:T(8,128)} %copy-done.1) | copy-start | bytes 2654212
  384.2 5.2 %copy-start.4 = (f32[24,96,96]{2,1,0:T(8,128)S(1)}, f32[24,96,96]{2,1,0:T(8,128)}, u32[]{:S(2)}) copy-start(f32[24,96,96]{2,1,0:T(8,128)} %copy-done.3) | copy-start | bytes 2654212
  400.9 26.7 %collective-permute-start.2 = (f32[24,96,192]{2,1,0:T(8,128)S(1)}, f32[24,96,192]{2,1,0:T(8,128)S(1)}, u32[]{:S(2)}, u32[]{:S(2)}) collective-permute-start(f32[24,96,192]{2,1,0:T(8,128)S(1)} %pad_maximum_fusion.6), channel_id=1, source_target_pairs={{0,28},{4,0},{8,4},{12,8},{16,12},{20,16},{24,20},{28,24},{1,29},{... | collective-permute-start | bytes 5308424 | tf_op jit(solution)/shard_map/ppermute | solution.py:20
  429.8 29.5 %collective-permute-start.3 = (f32[24,96,192]{2,1,0:T(8,128)}, f32[24,96,192]{2,1,0:T(8,128)}, u32[]{:S(2)}, u32[]{:S(2)}) collective-permute-start(f32[24,96,192]{2,1,0:T(8,128)} %maximum_add_fusion), channel_id=1, source_target_pairs={{0,28},{4,0},{8,4},{12,8},{16,12},{20,16},{24,20},{28,24},{1,29},{... | collective-permute-start | bytes 5308424 | tf_op jit(solution)/shard_map/ppermute | solution.py:20
  445.2 16.8 %copy-start.5 = (f32[24,96,96]{2,1,0:T(8,128)S(1)}, f32[24,96,96]{2,1,0:T(8,128)}, u32[]{:S(2)}) copy-start(f32[24,96,96]{2,1,0:T(8,128)} %get-tuple-element.9) | copy-start | bytes 2654212
  445.2 16.8 %copy-start.6 = (f32[24,96,96]{2,1,0:T(8,128)S(1)}, f32[24,96,96]{2,1,0:T(8,128)}, u32[]{:S(2)}) copy-start(f32[24,96,96]{2,1,0:T(8,128)} %get-tuple-element.8) | copy-start | bytes 2654212
  462.0 1.7 copy-start.12
  497.7 13.8 %copy-start.9 = (f32[1,24,9216]{2,1,0:T(8,128)S(1)}, f32[1,24,9216]{2,1,0:T(8,128)}, u32[]{:S(2)}) copy-start(f32[1,24,9216]{2,1,0:T(8,128)} %stack.30) | copy-start | bytes 2654212
  509.8 1.6 copy-start.10

commit v2 on v1

--- a/solution.py
+++ b/solution.py
@@ -11,7 +11,6 @@
 
 cell_edge = 41.05
 mixing = 0.25
-highest = lax.Precision.HIGHEST
 split = lax.Precision.HIGH
 
 
@@ -57,7 +56,7 @@
     def forward(density):
         volume = jnp.einsum("xyl,lm->xym", density, lane_table, precision=split)
         volume = jnp.einsum("xym,dy->xdm", volume, cas_values, precision=split)
-        return volume.reshape(slab_width, grid_count, column_width, lanes).transpose(1, 0, 2, 3)
+        return volume.reshape(density.shape[0], grid_count, column_width, lanes).transpose(1, 0, 2, 3)
 
     def column_solve(parts):
         volume = parts.reshape(G, column_width, lanes)
@@ -73,50 +72,88 @@
     def exchange(parts):
         return lax.all_to_all(parts, "grid", split_axis=0, concat_axis=0, tiled=True)
 
-    cubes = orbitals.reshape(band_count, slab_width, G, G)
-    own = [cubes[i] for i in range(band_count)]
-    wide_own = jnp.concatenate([own[i] for i in range(band_count) for _ in range(band_count)], axis=2)
+    def lanes_of(block):
+        rows = block.shape[1]
+        cubes = block.reshape(band_count, rows, G, G)
+        return [cubes[i] for i in range(band_count)]
 
-    visitors = []
-    current = jnp.concatenate(own, axis=2)
+    def repeated(bands):
+        return jnp.concatenate([band for band in bands for _ in range(band_count)], axis=2)
+
+    def tiled(bands):
+        return jnp.concatenate(list(bands) * band_count, axis=2)
+
+    head = slab_width // 3
+    bounds = [(0, head), (head, slab_width)]
+    raw = [orbitals[:, low:high] for low, high in bounds]
+    wide_own = [repeated(lanes_of(part)) for part in raw]
+
+    wide_visitors = []
     for hop_index in range(STEPS):
-        current = passed_along(current, "band", 1)
-        visitors.append(current)
-    sent = [
-        exchange(forward(wide_own * jnp.concatenate([visitor] * band_count, axis=2)))
-        for visitor in visitors
-    ]
-    returned = [exchange(column_solve(parts)) for parts in sent]
-    own_sum = [0.0] * band_count
-    returned_parts = []
-    for parts, visitor in zip(returned, visitors):
-        potential = backward(parts)
-        to_own = potential * jnp.concatenate([visitor] * band_count, axis=2)
-        to_visitor = potential * wide_own
-        back = []
-        for j in range(band_count):
+        raw = [passed_along(part, "band", 1) for part in raw]
+        wide_visitors.append([tiled(lanes_of(part)) for part in raw])
+
+    def joined(blocks):
+        return jnp.concatenate(blocks, axis=1)
+
+    sent = []
+    for hop_index in range(STEPS):
+        ready = [forward(o * v) for o, v in zip(wide_own, wide_visitors[hop_index])]
+        if hop_index == 0:
+            sent.append(joined([exchange(part) for part in ready]))
+        else:
+            sent.append(exchange(joined(ready)))
+    solved = [column_solve(parts) for parts in sent]
+    wide_own = jnp.concatenate(wide_own, axis=0)
+    wide_visitors = [jnp.concatenate(parts, axis=0) for parts in wide_visitors]
+
+    def band_sums(wide, by_own):
+        out = []
+        for kept in range(band_count):
             total = 0.0
-            for i in range(band_count):
-                at = (i * band_count + j) * G
-                total = total + to_visitor[:, :, at:at + G]
-            back.append(total)
-        for i in range(band_count):
-            for j in range(band_count):
-                at = (i * band_count + j) * G
-                own_sum[i] = own_sum[i] + to_own[:, :, at:at + G]
-        returned_parts.append(jnp.concatenate(back, axis=2))
-    carried = returned_parts[STEPS - 1]
+            for other in range(band_count):
+                pair = kept * band_count + other if by_own else other * band_count + kept
+                total = total + wide[:, :, pair * G:(pair + 1) * G]
+            out.append(total)
+        return out
+
+    def overlaps(wide_left, by_own, right):
+        rows = []
+        for a in range(band_count):
+            at = (a * band_count if by_own else a) * G
+            left = wide_left[:, :, at:at + G]
+            rows.append(jnp.stack([jnp.sum(left * right[b]) for b in range(band_count)]))
+        return jnp.stack(rows)
+
+    own_sum = None
+    own_overlap = 0.0
+    carried = None
+    carried_overlap = None
+    half = G // 2
+    held_back = None
     for hop_index in reversed(range(STEPS)):
-        carried = passed_along(carried, "band", -1)
-        if hop_index:
-            carried = carried + returned_parts[hop_index - 1]
-    images = -mixing * (
-        jnp.stack(own_sum) + jnp.stack([carried[:, :, i * G:(i + 1) * G] for i in range(band_count)])
+        parts = solved[hop_index]
+        if held_back is not None:
+            parts, held_back = lax.optimization_barrier((parts, held_back))
+        held_back = exchange(parts)
+        potential = backward(held_back)
+        to_own = band_sums(potential * wide_visitors[hop_index], True)
+        back = band_sums(potential * wide_own, False)
+        own_overlap = own_overlap + overlaps(wide_own, True, to_own)
+        back_overlap = overlaps(wide_visitors[hop_index], False, back)
+        own_sum = to_own if own_sum is None else [x + y for x, y in zip(own_sum, to_own)]
+        back = jnp.concatenate(back, axis=2)
+        back = jnp.concatenate([back[:, :half], back[:, half:]], axis=2)
+        carried = passed_along(back if carried is None else carried + back, "band", -1)
+        if carried_overlap is not None:
+            back_overlap = back_overlap + carried_overlap
+        carried_overlap = passed_along(back_overlap, "band", -1)
+    intersection = lax.psum((own_overlap + carried_overlap) * (-mixing / float(G * G * G)), "grid")
+    width = band_count * G
+    carried = jnp.concatenate([carried[:, :, :width], carried[:, :, width:]], axis=1)
+    images = -mixing * jnp.stack(
+        [own_sum[i] + carried[:, :, i * G:(i + 1) * G] for i in range(band_count)]
     )
-    partial_value = jnp.einsum(
-        "ixyz,jxyz->ij", cubes, images, precision=highest
-    ) / float(G * G * G)
-    intersection = lax.psum(partial_value, "grid")
     return (images.reshape(orbitals.shape), intersection)
 
 

time: 521 us -> 456 us (0.88)
  waiting for transfers between devices: 333 us -> 253 us
  matrix products: 85 us -> 53.2 us
  other arithmetic: 18.4 us -> 40.8 us
  local copies, waits for them, and re-layouts: 43.3 us -> 56.2 us
  starting transfers between devices: 23.6 us -> 36.1 us
    ppermute x4 -> x8, waiting for transfers between devices: 95.7 us -> 36.1 us  [passed_along(): lax.ppermute(x, axis, [(i, (i + by) % length) for i in range(length)])]
    dot_general x1 -> x0, matrix products: 32.5 us -> none  [shards(): jnp.einsum('ixyz,jxyz->ij', cubes, images, precision=highest)]
    all_to_all x4 -> x5, waiting for transfers between devices: 238 us -> 217 us  [exchange(): lax.all_to_all(parts, 'grid', split_axis=0, concat_axis=0, tiled=True)]
    concatenate x2 -> x8, other arithmetic: 2.79 us -> 16.2 us  [the longest x2 6.74 us: shards(): wide_visitors = [jnp.concatenate(parts, axis=0) for parts in wide_visitors]]
    squeeze x2 -> x12, local copies, waits for them, and re-layouts: 0.92 us -> 12.6 us  [lanes_of(): return [cubes[i] for i in range(band_count)]]
    another operation x0 -> x8, other arithmetic: none -> 10.4 us  [overlaps(): return jnp.stack(rows)]
    slice x1 -> x9, local copies, waits for them, and re-layouts: 1.55 us -> 11.5 us  [the longest x6 7.77 us: lanes_of(): return [cubes[i] for i in range(band_count)]]
    reduce_sum x0 -> x3, other arithmetic: none -> 9.87 us  [overlaps(): jnp.sum(left * right[b])]
  transfers between devices with their start and end apart: 8 -> 13, of which waited for: 8 -> 7; matrix products, arithmetic and copies ran while one was open for 12% -> 29% of each run, Pallas kernels for 0% -> 0%
where the time goes in v2:
time: 456 us; the launch traced here: 450 us
  waiting for transfers between devices  253 us (55%)
  local copies, waits for them, and re-layouts  56.2 us (12%)
  matrix products  53.2 us (12%)
  other arithmetic  40.8 us (9%)
  starting transfers between devices  36.1 us (8%)
  blocking collectives  9.45 us (2%)
    all_to_all x5, waiting for transfers between devices, exchange(): lax.all_to_all(parts, 'grid', split_axis=0, concat_axis=0, tiled=True)  217 us
    ppermute x8, waiting for transfers between devices, passed_along(): lax.ppermute(x, axis, [(i, (i + by) % length) for i in range(length)])  36.1 us
    all_to_all x5, starting transfers between devices, exchange(): lax.all_to_all(parts, 'grid', split_axis=0, concat_axis=0, tiled=True)  25.6 us
    dot_general x4, matrix products, forward(): volume = jnp.einsum('xyl,lm->xym', density, lane_table, precision=split)  19.7 us
    dot_general x2, matrix products, backward(): return jnp.einsum('xym,ml->xyl', volume, lane_table, precision=split)  13 us
    squeeze x12, local copies, waits for them, and re-layouts, lanes_of(): return [cubes[i] for i in range(band_count)]  12.6 us
    ppermute x8, starting transfers between devices, passed_along(): lax.ppermute(x, axis, [(i, (i + by) % length) for i in range(length)])  10.5 us
    another operation x8, other arithmetic, overlaps(): return jnp.stack(rows)  10.4 us
  transfers between devices with their start and end apart: 13, of which 7 were waited for; matrix products, arithmetic and copies ran while one was open for 29% of the time, Pallas kernels for 0%

profile of v2, /device:TPU:0, one launch (start us, length us, event | category | flops | bytes accessed | tf_op | source)
XLA Modules:
  0.0 450.3 jit_solution(2383379131516793979)
XLA Ops:
  0.6 2.5 slice.157
  4.5 2.6 collective-permute-start
  10.7 16.3 %collective-permute-done = f32[2,8,9216]{2,1,0:T(8,128)} collective-permute-done((f32[2,8,9216]{2,1,0:T(8,128)}, f32[2,8,9216]{2,1,0:T(8,128)}, u32[]{:S(2)}, u32[]{:S(2)}) %collective-permute-start) | collective-permute-done | bytes 589856 | tf_op jit(solution)/shard_map/ppermute | solution.py:19
  28.4 3.2 fusion.44
  33.7 5.6 %all-to-all-start.2 = ((f32[4,8,24,384]{3,2,1,0:T(8,128)}), f32[4,8,24,384]{3,2,1,0:T(8,128)S(1)}, u32[]{:S(2)}, u32[]{:S(2)}) async-start(f32[4,8,24,384]{3,2,1,0:T(8,128)} %bitcast.109), calls=%async_computation.2 | async-start | bytes 2359296 | tf_op jit(solution)/shard_map/all_to_all | solution.py:73
  43.4 3.2 fusion.37
  47.6 9.0 %collective-permute-done.3 = f32[2,16,9216]{2,1,0:T(8,128)} collective-permute-done((f32[2,16,9216]{2,1,0:T(8,128)}, f32[2,16,9216]{2,1,0:T(8,128)}, u32[]{:S(2)}, u32[]{:S(2)}) %collective-permute-start.3) | collective-permute-done | bytes 1179680 | tf_op jit(solution)/shard_map/ppermute | solution.py:19
  56.6 2.3 fusion.119
  58.9 2.3 squeeze.42
  61.2 2.3 squeeze.43
  63.5 6.3 %fusion.12 = f32[16,96,384]{2,1,0:T(8,128)S(1)} fusion(f32[384,384,1]{1,0,2:T(8,128)} %reshape.177, f32[16,96,96]{2,1,0:T(8,128)} %squeeze.43, f32[16,96,96]{2,1,0:T(8,128)} %squeeze.42, f32[16,96,96]{2,1,0:T(8,128)} %squeeze.41, f32[16,96,96]{2,1,0:T(8,128)S(1)} %squeeze.40), kind=kOutput, calls=%fused_computation.19 | convolution fusion | flops 1363083264 | bytes 5308416 | tf_op jit(solution)/shard_map/xyl,lm->xym/dot_general | solution.py:57
  71.3 2.0 pad_maximum_fusion
  74.4 5.3 %all-to-all-start = ((f32[4,24,24,384]{3,2,1,0:T(8,128)}), f32[4,24,24,384]{3,2,1,0:T(8,128)S(1)}, u32[]{:S(2)}, u32[]{:S(2)}) async-start(f32[4,24,24,384]{3,2,1,0:T(8,128)} %pad_maximum_fusion), calls=%async_computation | async-start | bytes 7077888 | tf_op jit(solution)/shard_map/all_to_all | solution.py:73
  79.6 2.4 fusion.118
  82.1 2.3 squeeze.46
  84.3 2.3 squeeze.47
  86.6 7.0 %fusion.19 = f32[16,96,384]{2,1,0:T(8,128)S(1)} fusion(f32[384,384,1]{1,0,2:T(8,128)} %reshape.177, f32[16,96,96]{2,1,0:T(8,128)} %squeeze.47, f32[16,96,96]{2,1,0:T(8,128)} %squeeze.46, f32[16,96,96]{2,1,0:T(8,128)} %squeeze.41, f32[16,96,96]{2,1,0:T(8,128)} %copy-done.7), kind=kOutput, calls=%fused_computation.27 | convolution fusion | flops 1363083264 | bytes 5308416 | tf_op jit(solution)/shard_map/xyl,lm->xym/dot_general | solution.py:57
  96.6 59.6 %all-to-all-done = f32[4,24,24,384]{3,2,1,0:T(8,128)S(1)} async-done(((f32[4,24,24,384]{3,2,1,0:T(8,128)}), f32[4,24,24,384]{3,2,1,0:T(8,128)S(1)}, u32[]{:S(2)}, u32[]{:S(2)}) %all-to-all-start) | async-done | bytes 3538976 | tf_op jit(solution)/shard_map/all_to_all | solution.py:73
  158.0 4.5 %all-to-all-start.3 = ((f32[4,16,24,384]{3,2,1,0:T(8,128)}), f32[4,16,24,384]{3,2,1,0:T(8,128)}, u32[]{:S(2)}, u32[]{:S(2)}) async-start(f32[4,16,24,384]{3,2,1,0:T(8,128)} %bitcast.118), calls=%async_computation.3 | async-start | bytes 4718592 | tf_op jit(solution)/shard_map/all_to_all | solution.py:73
  163.0 2.9 tile.4
  165.9 4.3 tile.10
  170.3 4.2 fusion.6
  176.4 3.8 copy.12
  180.2 35.6 %all-to-all-done.3 = f32[4,16,24,384]{3,2,1,0:T(8,128)} async-done(((f32[4,16,24,384]{3,2,1,0:T(8,128)}), f32[4,16,24,384]{3,2,1,0:T(8,128)}, u32[]{:S(2)}, u32[]{:S(2)}) %all-to-all-start.3) | async-done | bytes 2359328 | tf_op jit(solution)/shard_map/all_to_all | solution.py:73
  215.8 4.9 %all-to-all-start.1 = ((f32[4,24,24,384]{3,2,1,0:T(8,128)}), f32[4,24,24,384]{3,2,1,0:T(8,128)}, u32[]{:S(2)}, u32[]{:S(2)}) async-start(f32[4,24,24,384]{3,2,1,0:T(8,128)} %copy.12), calls=%async_computation.1 | async-start | bytes 7077888 | tf_op jit(solution)/shard_map/all_to_all | solution.py:73
  220.8 2.2 pad_maximum_fusion.1
  223.0 2.2 fusion.4
  225.2 3.6 fusion.8
  228.8 70.6 %all-to-all-done.1 = f32[4,24,24,384]{3,2,1,0:T(8,128)} async-done(((f32[4,24,24,384]{3,2,1,0:T(8,128)}), f32[4,24,24,384]{3,2,1,0:T(8,128)}, u32[]{:S(2)}, u32[]{:S(2)}) %all-to-all-start.1) | async-done | bytes 3538976 | tf_op jit(solution)/shard_map/all_to_all | solution.py:73
  299.4 5.9 %copy.17 = f32[4,24,24,384]{3,2,1,0:T(8,128)} copy(f32[4,24,24,384]{3,1,0,2:T(8,128)} %bitcast.115) | data formatting | bytes 7077888 | tf_op jit(solution)/shard_map/optimization_barrier | solution.py:137
  305.4 5.3 %all-to-all-start.4 = ((f32[4,24,24,384]{3,2,1,0:T(8,128)}), f32[4,24,24,384]{3,2,1,0:T(8,128)}, u32[]{:S(2)}, u32[]{:S(2)}) async-start(f32[4,24,24,384]{3,2,1,0:T(8,128)} %copy.17), calls=%async_computation.4 | async-start | bytes 7077888 | tf_op jit(solution)/shard_map/all_to_all | solution.py:73
  310.7 2.8 maximum_maximum_fusion.2
  313.6 4.0 maximum_maximum_fusion.1
  317.6 2.8 maximum_maximum_fusion
  320.3 2.4 copy.13
  322.8 2.0 fusion.61
  324.9 6.5 %fusion.112 = (f32[24,96,384]{2,1,0:T(8,128)S(1)}, f32[24,96,384]{2,1,0:T(8,128)S(1)}) fusion(f32[16,96,96]{2,1,0:T(8,128)S(1)} %copy-done.19, f32[16,96,96]{2,1,0:T(8,128)S(1)} %copy-done.18, f32[8,96,96]{2,1,0:T(8,128)S(1)} %copy-done.37, f32[8,96,96]{2,1,0:T(8,128)S(1)} %copy-done.35, f32[16,96,96]{2,1,0:T(8,128)S(1)} %copy-done.12, ...), kind=kOutput, calls=%fused_computation.182 | convolution fusion | flops 2052587520 | bytes 14745600 | tf_op jit(solution)/shard_map/xym,ml->xyl/dot_general | solution.py:70
  331.5 3.5 multiply_reduce_fusion.3
  338.2 51.1 %all-to-all-done.4 = f32[4,24,24,384]{3,2,1,0:T(8,128)} async-done(((f32[4,24,24,384]{3,2,1,0:T(8,128)}), f32[4,24,24,384]{3,2,1,0:T(8,128)}, u32[]{:S(2)}, u32[]{:S(2)}) %all-to-all-start.4) | async-done | bytes 3538976 | tf_op jit(solution)/shard_map/all_to_all | solution.py:73
  389.3 2.4 copy.18
  391.8 2.0 fusion.53
  394.2 6.5 %fusion.111 = (f32[24,96,384]{2,1,0:T(8,128)S(1)}, f32[24,96,384]{2,1,0:T(8,128)S(1)}) fusion(f32[16,96,96]{2,1,0:T(8,128)S(1)} %copy-done.17, f32[16,96,96]{2,1,0:T(8,128)S(1)} %copy-done.15, f32[8,96,96]{2,1,0:T(8,128)S(1)} %copy-done.33, f32[8,96,96]{2,1,0:T(8,128)S(1)} %copy-done.30, f32[16,96,96]{2,1,0:T(8,128)S(1)} %copy-done.13, ...), kind=kOutput, calls=%fused_computation.181 | convolution fusion | flops 2052587520 | bytes 14745600 | tf_op jit(solution)/shard_map/xym,ml->xyl/dot_general | solution.py:70
  403.0 2.0 fusion.27
  413.0 2.5 maximum_bitcast_fusion.4
  415.4 10.8 %collective-permute-done.6 = f32[2,2]{1,0:T(2,128)S(1)} collective-permute-done((f32[2,2]{1,0:T(2,128)S(1)}, f32[2,2]{1,0:T(2,128)S(1)}, u32[]{:S(2)}, u32[]{:S(2)}) %collective-permute-start.6) | collective-permute-done | bytes 48 | tf_op jit(solution)/shard_map/ppermute | solution.py:19
  426.2 2.9 collective-permute-start.7
  429.5 4.5 multiply_reduce_fusion.11
  436.7 9.4 %psum.7 = f32[2,2]{1,0:T(2,128)} all-reduce(f32[2,2]{1,0:T(2,128)S(1)} %fusion.74), channel_id=1, replica_groups=mesh['band'=8,'grid'=4] {'grid'}, use_global_device_ids=true, to_apply=%region_16.17 | all-reduce | flops 4 | bytes 32 | tf_op jit(solution)/shard_map/psum | solution.py:151
  (139 shorter events, 44.0 us)
Async XLA Ops:
  0.6 3.0 copy-start.4
  3.1 36.1 %collective-permute-start.2 = (f32[2,16,9216]{2,1,0:T(8,128)}, f32[2,16,9216]{2,1,0:T(8,128)}, u32[]{:S(2)}, u32[]{:S(2)}) collective-permute-start(f32[2,16,9216]{2,1,0:T(8,128)} %slice.157), channel_id=1, source_target_pairs={{0,4},{4,8},{8,12},{12,16},{16,20},{20,24},{24,28},{28,0},{1,5},{5... | collective-permute-start | bytes 3538952 | tf_op jit(solution)/shard_map/ppermute | solution.py:19
  4.5 22.5 %collective-permute-start = (f32[2,8,9216]{2,1,0:T(8,128)}, f32[2,8,9216]{2,1,0:T(8,128)}, u32[]{:S(2)}, u32[]{:S(2)}) collective-permute-start(f32[2,8,9216]{2,1,0:T(8,128)} %slice.152), channel_id=1, source_target_pairs={{0,4},{4,8},{8,12},{12,16},{16,20},{20,24},{24,28},{28,0},{1,5},{5... | collective-permute-start | bytes 1769480 | tf_op jit(solution)/shard_map/ppermute | solution.py:19
  7.5 56.0 %copy-start.7 = (f32[16,96,96]{2,1,0:T(8,128)}, f32[16,96,96]{2,1,0:T(8,128)S(1)}, u32[]{:S(2)}) copy-start(f32[16,96,96]{2,1,0:T(8,128)S(1)} %squeeze.40) | copy-start | bytes 1769476
  10.5 32.9 %copy-start.20 = (f32[8,96,96]{2,1,0:T(8,128)}, f32[8,96,96]{2,1,0:T(8,128)S(1)}, u32[]{:S(2)}) copy-start(f32[8,96,96]{2,1,0:T(8,128)S(1)} %squeeze.36) | copy-start | bytes 884740
  10.7 32.7 %copy-start.24 = (f32[8,96,96]{2,1,0:T(8,128)}, f32[8,96,96]{2,1,0:T(8,128)S(1)}, u32[]{:S(2)}) copy-start(f32[8,96,96]{2,1,0:T(8,128)S(1)} %squeeze.37) | copy-start | bytes 884740
  27.0 13.2 %collective-permute-start.1 = (f32[2,8,9216]{2,1,0:T(8,128)}, f32[2,8,9216]{2,1,0:T(8,128)}, u32[]{:S(2)}, u32[]{:S(2)}) collective-permute-start(f32[2,8,9216]{2,1,0:T(8,128)} %collective-permute-done), channel_id=1, source_target_pairs={{0,4},{4,8},{8,12},{12,16},{16,20},{20,24},{24,28},{28,0},{1,5},{5... | collective-permute-start | bytes 1769480 | tf_op jit(solution)/shard_map/ppermute | solution.py:19
  28.2 3.4 copy-start.28
  28.4 3.2 copy-start.31
  33.7 39.7 %all-to-all-start.2 = ((f32[4,8,24,384]{3,2,1,0:T(8,128)}), f32[4,8,24,384]{3,2,1,0:T(8,128)S(1)}, u32[]{:S(2)}, u32[]{:S(2)}) async-start(f32[4,8,24,384]{3,2,1,0:T(8,128)} %bitcast.109), calls=%async_computation.2 | async-start | bytes 2359296 | tf_op jit(solution)/shard_map/all_to_all | solution.py:73
  39.3 17.3 %collective-permute-start.3 = (f32[2,16,9216]{2,1,0:T(8,128)}, f32[2,16,9216]{2,1,0:T(8,128)}, u32[]{:S(2)}, u32[]{:S(2)}) collective-permute-start(f32[2,16,9216]{2,1,0:T(8,128)} %collective-permute-done.2), channel_id=1, source_target_pairs={{0,4},{4,8},{8,12},{12,16},{16,20},{20,24},{24,28},{28,0},{1,5},{5... | collective-permute-start | bytes 3538952 | tf_op jit(solution)/shard_map/ppermute | solution.py:19
  42.1 4.5 %copy-start.34 = (f32[8,96,96]{2,1,0:T(8,128)}, f32[8,96,96]{2,1,0:T(8,128)S(1)}, u32[]{:S(2)}) copy-start(f32[8,96,96]{2,1,0:T(8,128)S(1)} %squeeze.38) | copy-start | bytes 884740
  43.4 3.2 copy-start.36
  74.4 81.8 %all-to-all-start = ((f32[4,24,24,384]{3,2,1,0:T(8,128)}), f32[4,24,24,384]{3,2,1,0:T(8,128)S(1)}, u32[]{:S(2)}, u32[]{:S(2)}) async-start(f32[4,24,24,384]{3,2,1,0:T(8,128)} %pad_maximum_fusion), calls=%async_computation | async-start | bytes 7077888 | tf_op jit(solution)/shard_map/all_to_all | solution.py:73
  158.0 57.9 %all-to-all-start.3 = ((f32[4,16,24,384]{3,2,1,0:T(8,128)}), f32[4,16,24,384]{3,2,1,0:T(8,128)}, u32[]{:S(2)}, u32[]{:S(2)}) async-start(f32[4,16,24,384]{3,2,1,0:T(8,128)} %bitcast.118), calls=%async_computation.3 | async-start | bytes 4718592 | tf_op jit(solution)/shard_map/all_to_all | solution.py:73
  215.8 83.6 %all-to-all-start.1 = ((f32[4,24,24,384]{3,2,1,0:T(8,128)}), f32[4,24,24,384]{3,2,1,0:T(8,128)}, u32[]{:S(2)}, u32[]{:S(2)}) async-start(f32[4,24,24,384]{3,2,1,0:T(8,128)} %copy.12), calls=%async_computation.1 | async-start | bytes 7077888 | tf_op jit(solution)/shard_map/all_to_all | solution.py:73
  305.3 5.3 %copy-start.8 = (f32[16,96,96]{2,1,0:T(8,128)S(1)}, f32[16,96,96]{2,1,0:T(8,128)}, u32[]{:S(2)}) copy-start(f32[16,96,96]{2,1,0:T(8,128)} %copy-done.7) | copy-start | bytes 1769476
  305.3 5.3 %copy-start.11 = (f32[16,96,96]{2,1,0:T(8,128)S(1)}, f32[16,96,96]{2,1,0:T(8,128)}, u32[]{:S(2)}) copy-start(f32[16,96,96]{2,1,0:T(8,128)} %squeeze.41) | copy-start | bytes 1769476
  305.4 5.3 %copy-start.21 = (f32[8,96,96]{2,1,0:T(8,128)S(1)}, f32[8,96,96]{2,1,0:T(8,128)}, u32[]{:S(2)}) copy-start(f32[8,96,96]{2,1,0:T(8,128)} %copy-done.20) | copy-start | bytes 884740
  305.4 5.3 %copy-start.25 = (f32[8,96,96]{2,1,0:T(8,128)S(1)}, f32[8,96,96]{2,1,0:T(8,128)}, u32[]{:S(2)}) copy-start(f32[8,96,96]{2,1,0:T(8,128)} %copy-done.24) | copy-start | bytes 884740
  305.4 83.9 %all-to-all-start.4 = ((f32[4,24,24,384]{3,2,1,0:T(8,128)}), f32[4,24,24,384]{3,2,1,0:T(8,128)}, u32[]{:S(2)}, u32[]{:S(2)}) async-start(f32[4,24,24,384]{3,2,1,0:T(8,128)} %copy.17), calls=%async_computation.4 | async-start | bytes 7077888 | tf_op jit(solution)/shard_map/all_to_all | solution.py:73
  310.7 2.8 copy-start.14
  310.7 2.8 copy-start.16
  310.7 2.8 copy-start.29
  310.7 2.8 copy-start.32
  313.5 17.9 %copy-start = (f32[24,96,384]{2,1,0:T(8,128)}, f32[24,96,384]{2,1,0:T(8,128)S(1)}, u32[]{:S(2)}) copy-start(f32[24,96,384]{2,1,0:T(8,128)S(1)} %maximum_maximum_fusion.2) | copy-start | bytes 10616836
  313.5 4.0 copy-start.18
  313.5 4.0 copy-start.19
  313.5 4.0 copy-start.35
  313.6 4.0 copy-start.37
  322.8 2.1 copy-start.9
  322.8 2.1 copy-start.12
  337.1 65.9 %collective-permute-start.4 = (f32[24,48,384]{2,1,0:T(8,128)}, f32[24,48,384]{2,1,0:T(8,128)}, u32[]{:S(2)}, u32[]{:S(2)}) collective-permute-start(f32[24,48,384]{2,1,0:T(8,128)} %fusion.28), channel_id=1, source_target_pairs={{0,28},{4,0},{8,4},{12,8},{16,12},{20,16},{24,20},{28,24},{1,29},{... | collective-permute-start | bytes 5308424 | tf_op jit(solution)/shard_map/ppermute | solution.py:19
  391.7 2.1 copy-start.10
  391.7 2.1 copy-start.13
  391.7 2.1 copy-start.15
  391.7 2.1 copy-start.17
  391.8 2.1 copy-start.23
  391.8 2.1 copy-start.27
  391.8 2.1 copy-start.30
  391.8 2.2 copy-start.33
  391.8 2.4 copy-start.39
  394.2 6.5 %copy-start.3 = (f32[24,96,384]{2,1,0:T(8,128)S(1)}, f32[24,96,384]{2,1,0:T(8,128)}, u32[]{:S(2)}) copy-start(f32[24,96,384]{2,1,0:T(8,128)} %maximum_maximum_fusion.1) | copy-start | bytes 10616836
  405.1 24.0 %collective-permute-start.5 = (f32[24,48,384]{2,1,0:T(8,128)S(1)}, f32[24,48,384]{2,1,0:T(8,128)S(1)}, u32[]{:S(2)}, u32[]{:S(2)}) collective-permute-start(f32[24,48,384]{2,1,0:T(8,128)S(1)} %fusion.27), channel_id=1, source_target_pairs={{0,28},{4,0},{8,4},{12,8},{16,12},{20,16},{24,20},{28,24},{1,29},{... | collective-permute-start | bytes 5308424 | tf_op jit(solution)/shard_map/ppermute | solution.py:19
  408.8 17.4 %collective-permute-start.6 = (f32[2,2]{1,0:T(2,128)S(1)}, f32[2,2]{1,0:T(2,128)S(1)}, u32[]{:S(2)}, u32[]{:S(2)}) collective-permute-start(f32[2,2]{1,0:T(2,128)S(1)} %pad_maximum_fusion.11), channel_id=1, source_target_pairs={{0,28},{4,0},{8,4},{12,8},{16,12},{20,16},{24,20},{28,24},{1,29},{... | collective-permute-start | bytes 56 | tf_op jit(solution)/shard_map/ppermute | solution.py:19
  426.2 3.3 copy-start.1
  426.2 10.4 %collective-permute-start.7 = (f32[2,2]{1,0:T(2,128)S(1)}, f32[2,2]{1,0:T(2,128)S(1)}, u32[]{:S(2)}, u32[]{:S(2)}) collective-permute-start(f32[2,2]{1,0:T(2,128)S(1)} %maximum_add_fusion.1), channel_id=1, source_target_pairs={{0,28},{4,0},{8,4},{12,8},{16,12},{20,16},{24,20},{28,24},{1,29},{... | collective-permute-start | bytes 56 | tf_op jit(solution)/shard_map/ppermute | solution.py:19
  434.0 14.1 %copy-start.5 = (f32[24,96,96]{2,1,0:T(8,128)S(1)}, f32[24,96,96]{2,1,0:T(8,128)}, u32[]{:S(2)}) copy-start(f32[24,96,96]{2,1,0:T(8,128)} %get-tuple-element.30) | copy-start | bytes 2654212
  (5 other events, 9.0 us)

commit v3 on v2

--- a/solution.py
+++ b/solution.py
@@ -141,6 +141,7 @@
         back = band_sums(potential * wide_own, False)
         own_overlap = own_overlap + overlaps(wide_own, True, to_own)
         back_overlap = overlaps(wide_visitors[hop_index], False, back)
+        back, own_overlap, back_overlap = lax.optimization_barrier((back, own_overlap, back_overlap))
         own_sum = to_own if own_sum is None else [x + y for x, y in zip(own_sum, to_own)]
         back = jnp.concatenate(back, axis=2)
         back = jnp.concatenate([back[:, :half], back[:, half:]], axis=2)

time: 456 us -> 483 us (1.059)
  waiting for transfers between devices: 253 us -> 277 us
    ppermute x8, waiting for transfers between devices: 36.1 us -> 56.5 us  [passed_along(): lax.ppermute(x, axis, [(i, (i + by) % length) for i in range(length)])]
    another operation x8 -> x7, other arithmetic: 10.4 us -> 10.5 us  [overlaps(): return jnp.stack(rows)]
  transfers between devices with their start and end apart: 13 -> 13, of which waited for: 7 -> 9; matrix products, arithmetic and copies ran while one was open for 29% -> 24% of each run, Pallas kernels for 0% -> 0%
where the time goes in v3:
time: 483 us; the launch traced here: 478 us
  waiting for transfers between devices  277 us (57%)
  local copies, waits for them, and re-layouts  58.7 us (12%)
  matrix products  53.5 us (11%)
  other arithmetic  41.5 us (9%)
  starting transfers between devices  35.9 us (7%)
  blocking collectives  9.44 us (2%)
    all_to_all x5, waiting for transfers between devices, exchange(): lax.all_to_all(parts, 'grid', split_axis=0, concat_axis=0, tiled=True)  220 us
    ppermute x8, waiting for transfers between devices, passed_along(): lax.ppermute(x, axis, [(i, (i + by) % length) for i in range(length)])  56.5 us
    all_to_all x5, starting transfers between devices, exchange(): lax.all_to_all(parts, 'grid', split_axis=0, concat_axis=0, tiled=True)  25.6 us
    dot_general x4, matrix products, forward(): volume = jnp.einsum('xyl,lm->xym', density, lane_table, precision=split)  19.8 us
    dot_general x2, matrix products, backward(): return jnp.einsum('xym,ml->xyl', volume, lane_table, precision=split)  13.2 us
    squeeze x12, local copies, waits for them, and re-layouts, lanes_of(): return [cubes[i] for i in range(band_count)]  12.6 us
    another operation x7, other arithmetic, overlaps(): return jnp.stack(rows)  10.5 us
    ppermute x8, starting transfers between devices, passed_along(): lax.ppermute(x, axis, [(i, (i + by) % length) for i in range(length)])  10.3 us
  transfers between devices with their start and end apart: 13, of which 9 were waited for; matrix products, arithmetic and copies ran while one was open for 24% of the time, Pallas kernels for 0%

profile of v3, /device:TPU:0, one launch (start us, length us, event | category | flops | bytes accessed | tf_op | source)
XLA Modules:
  0.0 477.6 jit_solution(6125886986999386671)
XLA Ops:
  0.6 2.5 slice.157
  4.5 2.6 collective-permute-start
  10.7 16.3 %collective-permute-done = f32[2,8,9216]{2,1,0:T(8,128)} collective-permute-done((f32[2,8,9216]{2,1,0:T(8,128)}, f32[2,8,9216]{2,1,0:T(8,128)}, u32[]{:S(2)}, u32[]{:S(2)}) %collective-permute-start) | collective-permute-done | bytes 589856 | tf_op jit(solution)/shard_map/ppermute | solution.py:19
  28.4 3.2 fusion.44
  33.7 5.6 %all-to-all-start.2 = ((f32[4,8,24,384]{3,2,1,0:T(8,128)}), f32[4,8,24,384]{3,2,1,0:T(8,128)S(1)}, u32[]{:S(2)}, u32[]{:S(2)}) async-start(f32[4,8,24,384]{3,2,1,0:T(8,128)} %bitcast.109), calls=%async_computation.2 | async-start | bytes 2359296 | tf_op jit(solution)/shard_map/all_to_all | solution.py:73
  43.2 3.2 fusion.37
  47.3 9.0 %collective-permute-done.3 = f32[2,16,9216]{2,1,0:T(8,128)} collective-permute-done((f32[2,16,9216]{2,1,0:T(8,128)}, f32[2,16,9216]{2,1,0:T(8,128)}, u32[]{:S(2)}, u32[]{:S(2)}) %collective-permute-start.3) | collective-permute-done | bytes 1179680 | tf_op jit(solution)/shard_map/ppermute | solution.py:19
  56.3 2.3 fusion.117
  58.7 2.3 squeeze.42
  60.9 2.3 squeeze.43
  63.2 6.3 %fusion.12 = f32[16,96,384]{2,1,0:T(8,128)S(1)} fusion(f32[384,384,1]{1,0,2:T(8,128)} %reshape.177, f32[16,96,96]{2,1,0:T(8,128)} %squeeze.43, f32[16,96,96]{2,1,0:T(8,128)} %squeeze.42, f32[16,96,96]{2,1,0:T(8,128)} %squeeze.41, f32[16,96,96]{2,1,0:T(8,128)S(1)} %squeeze.40), kind=kOutput, calls=%fused_computation.19 | convolution fusion | flops 1363083264 | bytes 5308416 | tf_op jit(solution)/shard_map/xyl,lm->xym/dot_general | solution.py:57
  74.1 5.3 %all-to-all-start = ((f32[4,24,24,384]{3,2,1,0:T(8,128)}), f32[4,24,24,384]{3,2,1,0:T(8,128)S(1)}, u32[]{:S(2)}, u32[]{:S(2)}) async-start(f32[4,24,24,384]{3,2,1,0:T(8,128)} %pad_maximum_fusion), calls=%async_computation | async-start | bytes 7077888 | tf_op jit(solution)/shard_map/all_to_all | solution.py:73
  79.4 2.4 fusion.116
  81.8 2.3 squeeze.46
  84.1 2.3 squeeze.47
  86.4 7.1 %fusion.19 = f32[16,96,384]{2,1,0:T(8,128)S(1)} fusion(f32[384,384,1]{1,0,2:T(8,128)} %reshape.177, f32[16,96,96]{2,1,0:T(8,128)} %squeeze.47, f32[16,96,96]{2,1,0:T(8,128)} %squeeze.46, f32[16,96,96]{2,1,0:T(8,128)} %squeeze.41, f32[16,96,96]{2,1,0:T(8,128)} %copy-done.9), kind=kOutput, calls=%fused_computation.27 | convolution fusion | flops 1363083264 | bytes 5308416 | tf_op jit(solution)/shard_map/xyl,lm->xym/dot_general | solution.py:57
  96.5 59.5 %all-to-all-done = f32[4,24,24,384]{3,2,1,0:T(8,128)S(1)} async-done(((f32[4,24,24,384]{3,2,1,0:T(8,128)}), f32[4,24,24,384]{3,2,1,0:T(8,128)S(1)}, u32[]{:S(2)}, u32[]{:S(2)}) %all-to-all-start) | async-done | bytes 3538976 | tf_op jit(solution)/shard_map/all_to_all | solution.py:73
  157.9 4.5 all-to-all-start.3
  162.9 3.0 tile.4
  165.9 4.3 tile.10
  170.2 4.2 fusion.6
  176.4 3.9 copy.12
  180.3 35.5 %all-to-all-done.3 = f32[4,16,24,384]{3,2,1,0:T(8,128)} async-done(((f32[4,16,24,384]{3,2,1,0:T(8,128)}), f32[4,16,24,384]{3,2,1,0:T(8,128)}, u32[]{:S(2)}, u32[]{:S(2)}) %all-to-all-start.3) | async-done | bytes 2359328 | tf_op jit(solution)/shard_map/all_to_all | solution.py:73
  215.8 5.1 %all-to-all-start.1 = ((f32[4,24,24,384]{3,2,1,0:T(8,128)}), f32[4,24,24,384]{3,2,1,0:T(8,128)}, u32[]{:S(2)}, u32[]{:S(2)}) async-start(f32[4,24,24,384]{3,2,1,0:T(8,128)} %copy.12), calls=%async_computation.1 | async-start | bytes 7077888 | tf_op jit(solution)/shard_map/all_to_all | solution.py:73
  225.3 3.6 fusion.8
  228.9 70.6 %all-to-all-done.1 = f32[4,24,24,384]{3,2,1,0:T(8,128)} async-done(((f32[4,24,24,384]{3,2,1,0:T(8,128)}), f32[4,24,24,384]{3,2,1,0:T(8,128)}, u32[]{:S(2)}, u32[]{:S(2)}) %all-to-all-start.1) | async-done | bytes 3538976 | tf_op jit(solution)/shard_map/all_to_all | solution.py:73
  299.5 5.9 %copy.17 = f32[4,24,24,384]{3,2,1,0:T(8,128)} copy(f32[4,24,24,384]{3,1,0,2:T(8,128)} %bitcast.115) | data formatting | bytes 7077888 | tf_op jit(solution)/shard_map/optimization_barrier | solution.py:137
  305.5 5.1 %all-to-all-start.4 = ((f32[4,24,24,384]{3,2,1,0:T(8,128)}), f32[4,24,24,384]{3,2,1,0:T(8,128)}, u32[]{:S(2)}, u32[]{:S(2)}) async-start(f32[4,24,24,384]{3,2,1,0:T(8,128)} %copy.17), calls=%async_computation.4 | async-start | bytes 7077888 | tf_op jit(solution)/shard_map/all_to_all | solution.py:73
  310.6 4.1 maximum_maximum_fusion.2
  314.7 2.8 maximum_maximum_fusion
  317.4 2.4 copy.13
  322.0 6.5 %fusion.110 = (f32[24,96,384]{2,1,0:T(8,128)S(1)}, f32[24,96,384]{2,1,0:T(8,128)S(1)}) fusion(f32[16,96,96]{2,1,0:T(8,128)S(1)} %copy-done.19, f32[16,96,96]{2,1,0:T(8,128)S(1)} %copy-done.18, f32[8,96,96]{2,1,0:T(8,128)S(1)} %copy-done.37, f32[8,96,96]{2,1,0:T(8,128)S(1)} %copy-done.35, f32[16,96,96]{2,1,0:T(8,128)S(1)} %copy-done.14, ...), kind=kOutput, calls=%fused_computation.182 | convolution fusion | flops 2052587520 | bytes 14745600 | tf_op jit(solution)/shard_map/xym,ml->xyl/dot_general | solution.py:70
  328.5 3.4 multiply_reduce_fusion.11
  331.9 2.6 maximum_bitcast_fusion.2
  334.6 54.6 %all-to-all-done.4 = f32[4,24,24,384]{3,2,1,0:T(8,128)} async-done(((f32[4,24,24,384]{3,2,1,0:T(8,128)}), f32[4,24,24,384]{3,2,1,0:T(8,128)}, u32[]{:S(2)}, u32[]{:S(2)}) %all-to-all-start.4) | async-done | bytes 3538976 | tf_op jit(solution)/shard_map/all_to_all | solution.py:73
  389.2 2.4 copy.18
  394.1 6.7 %fusion.109 = (f32[24,96,384]{2,1,0:T(8,128)S(1)}, f32[24,96,384]{2,1,0:T(8,128)S(1)}) fusion(f32[16,96,96]{2,1,0:T(8,128)S(1)} %copy-done.17, f32[16,96,96]{2,1,0:T(8,128)S(1)} %copy-done.16, f32[8,96,96]{2,1,0:T(8,128)S(1)} %copy-done.24, f32[8,96,96]{2,1,0:T(8,128)S(1)} %copy-done.21, f32[16,96,96]{2,1,0:T(8,128)S(1)} %copy-done.15, ...), kind=kOutput, calls=%fused_computation.181 | convolution fusion | flops 2052587520 | bytes 14745600 | tf_op jit(solution)/shard_map/xym,ml->xyl/dot_general | solution.py:70
  400.9 2.9 multiply_reduce_fusion.7
  403.8 2.6 maximum_bitcast_fusion
  408.4 2.7 maximum_maximum_fusion.1
  413.2 2.7 maximum_bitcast_fusion.6
  415.9 2.6 maximum_bitcast_fusion.4
  418.9 9.6 %collective-permute-done.4 = f32[24,48,384]{2,1,0:T(8,128)S(1)} collective-permute-done((f32[24,48,384]{2,1,0:T(8,128)S(1)}, f32[24,48,384]{2,1,0:T(8,128)S(1)}, u32[]{:S(2)}, u32[]{:S(2)}) %collective-permute-start.4) | collective-permute-done | bytes 1769504 | tf_op jit(solution)/shard_map/ppermute | solution.py:19
  430.2 2.8 collective-permute-start.5
  433.1 20.3 %collective-permute-done.6 = f32[2,2]{1,0:T(2,128)S(1)} collective-permute-done((f32[2,2]{1,0:T(2,128)S(1)}, f32[2,2]{1,0:T(2,128)S(1)}, u32[]{:S(2)}, u32[]{:S(2)}) %collective-permute-start.6) | collective-permute-done | bytes 48 | tf_op jit(solution)/shard_map/ppermute | solution.py:19
  453.4 2.8 collective-permute-start.7
  457.5 9.4 %psum.7 = f32[2,2]{1,0:T(2,128)} all-reduce(f32[2,2]{1,0:T(2,128)S(1)} %add_multiply_fusion), channel_id=1, replica_groups=mesh['band'=8,'grid'=4] {'grid'}, use_global_device_ids=true, to_apply=%region_16.17 | all-reduce | flops 4 | bytes 32 | tf_op jit(solution)/shard_map/psum | solution.py:152
  469.6 3.6 fusion.33
  (140 shorter events, 48.1 us)
Async XLA Ops:
  0.6 3.0 copy-start.6
  3.1 36.2 %collective-permute-start.2 = (f32[2,16,9216]{2,1,0:T(8,128)}, f32[2,16,9216]{2,1,0:T(8,128)}, u32[]{:S(2)}, u32[]{:S(2)}) collective-permute-start(f32[2,16,9216]{2,1,0:T(8,128)} %slice.157), channel_id=1, source_target_pairs={{0,4},{4,8},{8,12},{12,16},{16,20},{20,24},{24,28},{28,0},{1,5},{5... | collective-permute-start | bytes 3538952 | tf_op jit(solution)/shard_map/ppermute | solution.py:19
  4.5 22.5 %collective-permute-start = (f32[2,8,9216]{2,1,0:T(8,128)}, f32[2,8,9216]{2,1,0:T(8,128)}, u32[]{:S(2)}, u32[]{:S(2)}) collective-permute-start(f32[2,8,9216]{2,1,0:T(8,128)} %slice.152), channel_id=1, source_target_pairs={{0,4},{4,8},{8,12},{12,16},{16,20},{20,24},{24,28},{28,0},{1,5},{5... | collective-permute-start | bytes 1769480 | tf_op jit(solution)/shard_map/ppermute | solution.py:19
  7.5 55.7 %copy-start.9 = (f32[16,96,96]{2,1,0:T(8,128)}, f32[16,96,96]{2,1,0:T(8,128)S(1)}, u32[]{:S(2)}) copy-start(f32[16,96,96]{2,1,0:T(8,128)S(1)} %squeeze.40) | copy-start | bytes 1769476
  10.5 32.6 %copy-start.26 = (f32[8,96,96]{2,1,0:T(8,128)}, f32[8,96,96]{2,1,0:T(8,128)S(1)}, u32[]{:S(2)}) copy-start(f32[8,96,96]{2,1,0:T(8,128)S(1)} %squeeze.36) | copy-start | bytes 884740
  10.7 32.5 %copy-start.30 = (f32[8,96,96]{2,1,0:T(8,128)}, f32[8,96,96]{2,1,0:T(8,128)S(1)}, u32[]{:S(2)}) copy-start(f32[8,96,96]{2,1,0:T(8,128)S(1)} %squeeze.37) | copy-start | bytes 884740
  27.0 12.9 %collective-permute-start.1 = (f32[2,8,9216]{2,1,0:T(8,128)}, f32[2,8,9216]{2,1,0:T(8,128)}, u32[]{:S(2)}, u32[]{:S(2)}) collective-permute-start(f32[2,8,9216]{2,1,0:T(8,128)} %collective-permute-done), channel_id=1, source_target_pairs={{0,4},{4,8},{8,12},{12,16},{16,20},{20,24},{24,28},{28,0},{1,5},{5... | collective-permute-start | bytes 1769480 | tf_op jit(solution)/shard_map/ppermute | solution.py:19
  28.2 3.4 copy-start.20
  28.4 3.2 copy-start.23
  33.7 39.4 %all-to-all-start.2 = ((f32[4,8,24,384]{3,2,1,0:T(8,128)}), f32[4,8,24,384]{3,2,1,0:T(8,128)S(1)}, u32[]{:S(2)}, u32[]{:S(2)}) async-start(f32[4,8,24,384]{3,2,1,0:T(8,128)} %bitcast.109), calls=%async_computation.2 | async-start | bytes 2359296 | tf_op jit(solution)/shard_map/all_to_all | solution.py:73
  39.3 17.0 %collective-permute-start.3 = (f32[2,16,9216]{2,1,0:T(8,128)}, f32[2,16,9216]{2,1,0:T(8,128)}, u32[]{:S(2)}, u32[]{:S(2)}) collective-permute-start(f32[2,16,9216]{2,1,0:T(8,128)} %collective-permute-done.2), channel_id=1, source_target_pairs={{0,4},{4,8},{8,12},{12,16},{16,20},{20,24},{24,28},{28,0},{1,5},{5... | collective-permute-start | bytes 3538952 | tf_op jit(solution)/shard_map/ppermute | solution.py:19
  41.9 4.5 copy-start.34
  43.1 3.2 copy-start.36
  74.1 81.9 %all-to-all-start = ((f32[4,24,24,384]{3,2,1,0:T(8,128)}), f32[4,24,24,384]{3,2,1,0:T(8,128)S(1)}, u32[]{:S(2)}, u32[]{:S(2)}) async-start(f32[4,24,24,384]{3,2,1,0:T(8,128)} %pad_maximum_fusion), calls=%async_computation | async-start | bytes 7077888 | tf_op jit(solution)/shard_map/all_to_all | solution.py:73
  157.9 57.9 %all-to-all-start.3 = ((f32[4,16,24,384]{3,2,1,0:T(8,128)}), f32[4,16,24,384]{3,2,1,0:T(8,128)}, u32[]{:S(2)}, u32[]{:S(2)}) async-start(f32[4,16,24,384]{3,2,1,0:T(8,128)} %bitcast.118), calls=%async_computation.3 | async-start | bytes 4718592 | tf_op jit(solution)/shard_map/all_to_all | solution.py:73
  215.8 83.8 %all-to-all-start.1 = ((f32[4,24,24,384]{3,2,1,0:T(8,128)}), f32[4,24,24,384]{3,2,1,0:T(8,128)}, u32[]{:S(2)}, u32[]{:S(2)}) async-start(f32[4,24,24,384]{3,2,1,0:T(8,128)} %copy.12), calls=%async_computation.1 | async-start | bytes 7077888 | tf_op jit(solution)/shard_map/all_to_all | solution.py:73
  305.4 5.1 %copy-start.10 = (f32[16,96,96]{2,1,0:T(8,128)S(1)}, f32[16,96,96]{2,1,0:T(8,128)}, u32[]{:S(2)}) copy-start(f32[16,96,96]{2,1,0:T(8,128)} %copy-done.9) | copy-start | bytes 1769476
  305.4 5.1 %copy-start.13 = (f32[16,96,96]{2,1,0:T(8,128)S(1)}, f32[16,96,96]{2,1,0:T(8,128)}, u32[]{:S(2)}) copy-start(f32[16,96,96]{2,1,0:T(8,128)} %squeeze.41) | copy-start | bytes 1769476
  305.4 5.1 %copy-start.27 = (f32[8,96,96]{2,1,0:T(8,128)S(1)}, f32[8,96,96]{2,1,0:T(8,128)}, u32[]{:S(2)}) copy-start(f32[8,96,96]{2,1,0:T(8,128)} %copy-done.26) | copy-start | bytes 884740
  305.4 5.1 %copy-start.31 = (f32[8,96,96]{2,1,0:T(8,128)S(1)}, f32[8,96,96]{2,1,0:T(8,128)}, u32[]{:S(2)}) copy-start(f32[8,96,96]{2,1,0:T(8,128)} %copy-done.30) | copy-start | bytes 884740
  305.5 83.7 %all-to-all-start.4 = ((f32[4,24,24,384]{3,2,1,0:T(8,128)}), f32[4,24,24,384]{3,2,1,0:T(8,128)}, u32[]{:S(2)}, u32[]{:S(2)}) async-start(f32[4,24,24,384]{3,2,1,0:T(8,128)} %copy.17), calls=%async_computation.4 | async-start | bytes 7077888 | tf_op jit(solution)/shard_map/all_to_all | solution.py:73
  310.6 4.1 copy-start.18
  310.6 4.1 copy-start.19
  310.6 4.1 copy-start.35
  310.6 4.1 copy-start.37
  319.9 2.1 copy-start.11
  319.9 2.1 copy-start.14
  319.9 2.1 copy-start.28
  319.9 2.1 copy-start.32
  319.9 2.1 copy-start.38
  391.6 2.1 copy-start.12
  391.6 2.1 copy-start.15
  391.6 2.1 copy-start.16
  391.6 2.1 copy-start.17
  391.6 2.1 copy-start.21
  391.6 2.1 copy-start.24
  391.7 2.1 copy-start.29
  391.7 2.2 copy-start.33
  391.7 2.4 copy-start.39
  394.1 6.7 %copy-start.5 = (f32[24,96,384]{2,1,0:T(8,128)S(1)}, f32[24,96,384]{2,1,0:T(8,128)}, u32[]{:S(2)}) copy-start(f32[24,96,384]{2,1,0:T(8,128)} %maximum_maximum_fusion.2) | copy-start | bytes 10616836
  400.8 3.0 copy-start
  400.8 5.6 %copy-start.3 = (f32[24,96,96]{2,1,0:T(8,128)S(1)}, f32[24,96,96]{2,1,0:T(8,128)}, u32[]{:S(2)}) copy-start(f32[24,96,96]{2,1,0:T(8,128)} %get-tuple-element.13) | copy-start | bytes 2654212
  400.9 5.6 %copy-start.4 = (f32[24,96,96]{2,1,0:T(8,128)S(1)}, f32[24,96,96]{2,1,0:T(8,128)}, u32[]{:S(2)}) copy-start(f32[24,96,96]{2,1,0:T(8,128)} %get-tuple-element.12) | copy-start | bytes 2654212
  407.4 21.1 %collective-permute-start.4 = (f32[24,48,384]{2,1,0:T(8,128)S(1)}, f32[24,48,384]{2,1,0:T(8,128)S(1)}, u32[]{:S(2)}, u32[]{:S(2)}) collective-permute-start(f32[24,48,384]{2,1,0:T(8,128)S(1)} %fusion.28), channel_id=1, source_target_pairs={{0,28},{4,0},{8,4},{12,8},{16,12},{20,16},{24,20},{28,24},{1,29},{... | collective-permute-start | bytes 5308424 | tf_op jit(solution)/shard_map/ppermute | solution.py:19
  430.2 36.7 %collective-permute-start.5 = (f32[24,48,384]{2,1,0:T(8,128)}, f32[24,48,384]{2,1,0:T(8,128)}, u32[]{:S(2)}, u32[]{:S(2)}) collective-permute-start(f32[24,48,384]{2,1,0:T(8,128)} %fusion.27), channel_id=1, source_target_pairs={{0,28},{4,0},{8,4},{12,8},{16,12},{20,16},{24,20},{28,24},{1,29},{... | collective-permute-start | bytes 5308424 | tf_op jit(solution)/shard_map/ppermute | solution.py:19
  433.0 20.4 %collective-permute-start.6 = (f32[2,2]{1,0:T(2,128)S(1)}, f32[2,2]{1,0:T(2,128)S(1)}, u32[]{:S(2)}, u32[]{:S(2)}) collective-permute-start(f32[2,2]{1,0:T(2,128)S(1)} %pad_maximum_fusion.12), channel_id=1, source_target_pairs={{0,28},{4,0},{8,4},{12,8},{16,12},{20,16},{24,20},{28,24},{1,29},{... | collective-permute-start | bytes 56 | tf_op jit(solution)/shard_map/ppermute | solution.py:19
  453.4 4.1 collective-permute-start.7
  466.9 2.7 copy-start.1
  (5 other events, 8.1 us)
